TPU v7x, 512 devices: a whole 4x8x8 slice. The times are simulated.
512 devices in a mesh: user: 32 (over x, y), item: 16 (over z, core).
Axes of the slice: x: 4, y: 8, z: 8, core: 2. Of those that a mesh axis runs over, the one named last changes fastest.
Arguments:
- user_emb: bfloat16 [32768, 256], P(('user', 'item')), may hold values from -109 to 109
- item_codes: int32 [3, 32768], P(None, ('item', 'user')), may hold values from 0 to 255
- targets: int32 [32768], P(('user', 'item')), may hold values from 0 to 32767
- codebook: bfloat16 [3, 256, 256], replicated, may hold values from -6 to 6
Outputs:
- grad_user: float32 [32768, 256], P(('user', 'item'))
- grad_codebook: float32 [3, 256, 256], replicated
- loss: float32 [], replicated
All inputs are finite; a program needn't handle non-finite values.
Results may differ from a plain program's by a relative error of at most 0.0015.
The roundings to bfloat16 on the way count: a program that leaves them out, or rounds other values in their place, can miss the bound.
Values may be sent and summed in bfloat16 or wider, within the bound.
A program may use at most 64 MiB of HBM per device.

v0:
```python
import jax
import jax.numpy as jnp
from jax import lax
from jax.sharding import PartitionSpec as P

D = 256


def decode_items(codes, codebook):
    summed = jnp.zeros((codes.shape[1], codebook.shape[2]), jnp.float32)
    for level_idx in range(codebook.shape[0]):
        onehot = (
            codes[level_idx][:, None] == jnp.arange(codebook.shape[1], dtype=jnp.int32)[None, :]
        ).astype(jnp.bfloat16)
        summed = summed + jnp.dot(onehot, codebook[level_idx], preferred_element_type=jnp.float32)
    return summed


def split_three(grads):
    high = lax.optimization_barrier(grads.astype(jnp.bfloat16))
    rest = grads - high.astype(jnp.float32)
    middle = lax.optimization_barrier(rest.astype(jnp.bfloat16))
    low = (rest - middle.astype(jnp.float32)).astype(jnp.bfloat16)
    return (high, middle, low)


def codebook_terms(codes, grads, codebook):
    pieces = split_three(grads)
    levels_out = []
    for level_idx in range(codebook.shape[0]):
        onehot = (
            codes[level_idx][:, None] == jnp.arange(codebook.shape[1], dtype=jnp.int32)[None, :]
        ).astype(jnp.bfloat16)
        total = jnp.zeros((codebook.shape[1], grads.shape[1]), jnp.float32)
        for piece in pieces:
            total = total + lax.dot_general(
                onehot, piece, (((0,), (0,)), ((), ())), preferred_element_type=jnp.float32
            )
        levels_out.append(total)
    return jnp.stack(levels_out)


def shards(user_emb, item_codes, targets, codebook):
    logit_scale = D ** (-0.5)
    own_users = user_emb.shape[0]
    block_users, block_targets = (
        lax.all_gather(user_emb, "item", axis=0, tiled=True),
        lax.all_gather(targets, "item", axis=0, tiled=True),
    )
    own_vectors = decode_items(item_codes, codebook).astype(jnp.bfloat16)
    block_items = lax.all_gather(own_vectors, "user", axis=0, tiled=True)
    first_col = lax.axis_index("item") * block_items.shape[0]
    columns = first_col + jnp.arange(block_items.shape[0], dtype=jnp.int32)
    logits = (
        lax.dot_general(
            block_users, block_items, (((1,), (1,)), ((), ())), preferred_element_type=jnp.float32
        )
        * logit_scale
    )
    is_target = block_targets[:, None] == columns[None, :]
    local_max = jnp.max(logits, axis=1)
    local_pos = jnp.sum(jnp.where(is_target, logits, 0.0), axis=1)
    row_max = lax.pmax(local_max, "item")
    local_sum = jnp.sum(jnp.exp(logits - row_max[:, None]), axis=1)
    row_sum, pos_logit = lax.psum((local_sum, local_pos), "item")
    lse = row_max + jnp.log(row_sum)
    dlogits = (jnp.exp(logits - lse[:, None]) - is_target.astype(jnp.float32)).astype(jnp.bfloat16)
    grad_user = lax.psum_scatter(
        jnp.dot(dlogits, block_items, preferred_element_type=jnp.float32) * logit_scale,
        "item",
        scatter_dimension=0,
        tiled=True,
    )
    own_grad = lax.psum_scatter(
        lax.dot_general(
            dlogits, block_users, (((0,), (0,)), ((), ())), preferred_element_type=jnp.float32
        )
        * logit_scale,
        "user",
        scatter_dimension=0,
        tiled=True,
    )
    cb_terms = codebook_terms(item_codes, own_grad, codebook)
    row_losses = lax.dynamic_slice_in_dim(
        lse - pos_logit, lax.axis_index("item") * own_users, own_users, 0
    )
    grad_codebook, loss_sum = lax.psum((cb_terms, jnp.sum(row_losses)), ("user", "item"))
    loss = loss_sum / (own_users * lax.axis_size("item") * lax.axis_size("user"))
    return (grad_user, grad_codebook, loss)


def solution(mesh):
    return jax.shard_map(
        shards,
        mesh=mesh,
        in_specs=(P(("user", "item"), None), P(None, ("item", "user")), P(("user", "item")), P()),
        out_specs=(P(("user", "item"), None), P(), P()),
        check_vma=False,
    )
```

profile of v0, /device:TPU:1, one launch (start us, length us, event | category | flops | bytes accessed | tf_op | source)
XLA Modules:
  0.0 733.9 jit_solution(12960099865926417259)
XLA Ops:
  8.0 1.1 fusion.12
  9.1 1.1 convolution_add_fusion.7
  10.2 1.7 fusion.9
  12.0 1.3 dynamic-slice
  13.9 0.9 dynamic-update-slice
  14.8 17.9 %all-reduce = s32[1024]{0:T(1024)S(1)} all-reduce(s32[1024]{0:T(1024)S(1)} %dynamic-update-slice), channel_id=1, replica_groups=mesh['user'=32,'item'=16] {'item'}, use_global_device_ids=true, to_apply=%add | all-reduce | flops 1024 | bytes 8192
  32.7 19.6 %all_gather.10 = bf16[1024,256]{1,0:T(8,128)(2,1)S(1)} all-gather(bf16[64,256]{1,0:T(8,128)(2,1)} %param.4), channel_id=1, replica_groups=mesh['user'=32,'item'=16] {'item'}, dimensions={0}, use_global_device_ids=true | all-gather | bytes 557056 | tf_op jit(solution)/shard_map/all_gather | solution.py:47
  52.3 42.3 %all-gather.2.cloned.1.call-done = bf16[2048,256]{1,0:T(8,128)(2,1)} async-done(((bf16[64,256]{1,0:T(8,128)(2,1)}), bf16[2048,256]{1,0:T(8,128)(2,1)}) %all-gather.2.cloned.1.call-update) | async-done | bytes 1048592 | tf_op jit(solution)/shard_map/all_gather | solution.py:51
  94.6 5.7 multiply_reduce_fusion
  100.3 29.0 %pmax.7 = f32[1024]{0:T(1024)S(1)} all-reduce(f32[1024]{0:T(1024)S(1)} %get-tuple-element.12), channel_id=1, replica_groups=mesh['user'=32,'item'=16] {'item'}, use_global_device_ids=true, to_apply=%region_1.2 | all-reduce | flops 1024 | bytes 8192 | tf_op jit(solution)/shard_map/pmax | solution.py:63
  129.3 4.6 fusion.2
  133.9 23.5 %all-reduce.1 = (f32[1024]{0:T(1024)S(1)}, f32[1024]{0:T(1024)S(1)}) all-reduce(f32[1024]{0:T(1024)S(1)} %get-tuple-element.4, f32[1024]{0:T(1024)S(1)} %get-tuple-element.3), channel_id=1, replica_groups=mesh['user'=32,'item'=16] {'item'}, use_global_device_ids=true, to_apply=%region_3.4 | all-reduce | flops 2048 | bytes 16384 | tf_op jit(solution)/shard_map/psum | solution.py:65
  157.5 4.6 fusion.1
  162.1 1.9 copy-done
  164.0 2.6 convolution_multiply_fusion
  166.7 4.5 convolution_multiply_fusion.1
  171.2 209.3 %reduce-scatter.5.cloned.1.call-done = f32[64,256]{1,0:T(8,128)} async-done(((f32[2048,256]{1,0:T(8,128)}), f32[64,256]{1,0:T(8,128)}) %reduce-scatter.5.cloned.1.call-update) | async-done | bytes 65552 | tf_op jit(solution)/shard_map/reduce_scatter | solution.py:74
  380.5 0.8 convert_element_type.33
  381.3 0.8 fusion.20
  382.2 0.9 subtract_convert_fusion
  385.8 0.9 pad_maximum_fusion
  387.4 103.3 %psum.31 = f32[]{:T(128)} all-reduce(f32[]{:T(128)} %dynamic-slice_reduce_fusion), channel_id=1, replica_groups=mesh['user'=32,'item'=16] {'user','item'}, use_global_device_ids=true, to_apply=%region_10.11 | all-reduce | flops 1 | bytes 8 | tf_op jit(solution)/shard_map/psum | solution.py:87
  491.4 232.7 %all-reduce.4.cloned.1.call-done = f32[3,256,256]{2,1,0:T(8,128)} async-done(((f32[3,256,256]{2,1,0:T(8,128)}), f32[3,256,256]{2,1,0:T(8,128)}) %all-reduce.4.cloned.1.call-update) | async-done | bytes 786448 | tf_op jit(solution)/shard_map/psum | solution.py:87
  724.1 2.1 copy.9
  (26 shorter events, 4.4 us)
Async XLA Ops:
  7.2 87.4 %all-gather.2.cloned.1.call-start = ((), (), s32[]{:S(2)}) async-start(), calls=%async_computation.2 | async-start | bytes 1081344 | tf_op jit(solution)/shard_map/all_gather | solution.py:51
  11.9 368.6 %reduce-scatter.5.cloned.1.call-start = ((), (), s32[]{:S(2)}) async-start(), calls=%async_computation.4 | async-start | bytes 2162688 | tf_op jit(solution)/shard_map/reduce_scatter | solution.py:74
  157.5 9.2 %copy-start.1 = (bf16[2048,256]{1,0:T(8,128)(2,1)S(1)}, bf16[2048,256]{1,0:T(8,128)(2,1)}, u32[]{:S(2)}) copy-start(bf16[2048,256]{1,0:T(8,128)(2,1)} %all-gather.2.cloned.1.call-done) | copy-start | bytes 3145732
  162.1 1.9 copy-start
  166.6 324.8 %reduce-scatter.3.cloned.1.call-start = ((), (), s32[]{:S(2)}) async-start(), calls=%async_computation.3 | async-start | bytes 1114112 | tf_op jit(solution)/shard_map/reduce_scatter | solution.py:68
  171.2 552.9 %all-reduce.4.cloned.1.call-start = ((), (), s32[]{:S(2)}) async-start(), calls=%async_computation.5 | async-start | bytes 1572864 | tf_op jit(solution)/shard_map/psum | solution.py:87
Sparse Core Ops, SparseCore 0:
  12.1 82.4 all-gather.1
  166.8 213.6 reduce-scatter.4
  384.1 61.8 reduce-scatter.2
  451.5 272.6 all-reduce.3
where the time goes:
time: 735 us; the launch traced here: 734 us
  waiting for transfers between devices  484 us (66%)
  blocking collectives  193 us (26%)
  matrix products  19.3 us (3%)
  between operations  16.4 us (2%)
  other arithmetic  13.4 us (2%)
    psum x1, waiting for transfers between devices, shards(): lax.psum((cb_terms, jnp.sum(row_losses)), ('user', 'item'))  233 us
    reduce_scatter x1, waiting for transfers between devices, shards(): lax.psum_scatter(lax.dot_general(dlogits, block_users, (((0,), (0,)), (()...  209 us
    psum x1, blocking collectives, shards(): lax.psum((cb_terms, jnp.sum(row_losses)), ('user', 'item'))  103 us
    all_gather x1, waiting for transfers between devices, shards(): block_items = lax.all_gather(own_vectors, 'user', axis=0, tiled=True)  42.3 us
    pmax x1, blocking collectives, shards(): row_max = lax.pmax(local_max, 'item')  29 us
    psum x1, blocking collectives, shards(): row_sum, pos_logit = lax.psum((local_sum, local_pos), 'item')  23.5 us
    all_gather x1, blocking collectives, shards(): lax.all_gather(user_emb, 'item', axis=0, tiled=True)  19.6 us
    unnamed x1, blocking collectives  17.9 us
  transfers between devices with their start and end apart: 4, of which 3 were waited for; matrix products, arithmetic and copies ran while one was open for 2% of the time, Pallas kernels for 0%

commit v1 on v0

v1 whole, which is shorter than its diff:
```python
import jax
import jax.numpy as jnp
from jax import lax
from jax.experimental import pallas as pl
from jax.experimental.pallas import tpu as pltpu
from jax.sharding import PartitionSpec as P

MESH = pl.DeviceIdType.MESH
NX, NY, NZ = 4, 8, 8
D = 256
K = 256
LEVELS = 3
OWN = 64
GROUP = 4
BLK = GROUP * OWN
ITEMS = 8192
CHUNK = 1024
STEPS = ITEMS // CHUNK
LANES = 128
SUBS = CHUNK // LANES
USERS = 32768
F32 = jnp.float32
BF16 = jnp.bfloat16


def dot(a, b):
    return jnp.dot(a, b, preferred_element_type=F32)


def dot_t(a, b):
    return lax.dot_general(a, b, (((1,), (1,)), ((), ())), preferred_element_type=F32)


def kernel(
    ue_hbm, codes_hbm, tg_hbm, cb_hbm, gu_ref, gc_ref, loss_ref,
    ub, us, cd, tg, slab, zb, yb, xb, tgb, cb, cbt, iota_k, col,
    oh, vt, lg, dl, mrun, srun, stat, lsec, tcol, pos,
    wacc, cbuf, dbuf, part, xr, ys, yr, zr, ay, fin,
    gus, gur, lv, ld, lx, ly, lz,
    loc, zs, zrs, tss, trs, uss, urs, yss, yrs, xss, xrs, sss, srs,
    ds, dr, xs1, xr1, ys1, yr1, zs1, zr1, ys2, yr2, xs2, xr2, ds2, dr2, gss, grs,
    lds, ldr, lxs, lxr, lys, lyr, lzs, lzr,
):
    u, i = lax.axis_index("user"), lax.axis_index("item")
    x, y = u // NY, lax.rem(u, NY)
    z, c = i // 2, lax.rem(i, 2)
    r = lax.rem(i, GROUP)
    sg = 1 - 2 * lax.rem(z, 2)

    def dev(x_, y_, z_, c_):
        return (x_ * NY + y_, z_ * 2 + c_)

    def xpeer(d):
        return lax.rem(x + d, NX)

    def ypeer(d):
        return lax.rem(y + d, NY)

    def zpeer(d):
        return lax.rem(z + d + NZ, NZ)

    zn = z + sg

    barrier = pltpu.get_barrier_semaphore()
    peers = [dev(xpeer(d), y, z, c) for d in range(1, NX)]
    peers += [dev(x, ypeer(d), z, c) for d in range(1, NY)]
    peers += [dev(x, y, zpeer(d), c) for d in range(1, NZ)]
    peers += [dev(x, y, z, 1 - c), dev(x, y, zn, 1 - c)]
    for peer in peers:
        pl.semaphore_signal(barrier, inc=1, device_id=peer, device_id_type=MESH)

    def send(src, dst, ss, rs, to):
        copy = pltpu.make_async_remote_copy(
            src_ref=src, dst_ref=dst, send_sem=ss, recv_sem=rs, device_id=to, device_id_type=MESH
        )
        copy.start()
        return copy

    own_rows = pl.ds(pl.multiple_of(r * OWN, OWN), OWN)
    loads = [
        pltpu.make_async_copy(codes_hbm, cd, loc.at[0]),
        pltpu.make_async_copy(tg_hbm, tg, loc.at[1]),
        pltpu.make_async_copy(ue_hbm, ub.at[own_rows, :], loc.at[2]),
        pltpu.make_async_copy(cb_hbm, cb, loc.at[3]),
    ]
    for load in loads:
        load.start()
    for load in loads[:3]:
        load.wait()

    own = cd[...].astype(F32)
    low = jnp.concatenate([own, jnp.zeros((LEVELS, OWN), F32)], axis=1)
    high = jnp.concatenate([jnp.zeros((LEVELS, OWN), F32), own], axis=1)
    none3 = jnp.zeros((3, LANES), F32)
    none2 = jnp.zeros((2, LANES), F32)
    slab[0] = jnp.concatenate([low, none3, none2], axis=0)
    slab[1] = jnp.concatenate([high, none3, none2], axis=0)
    slab[2] = jnp.concatenate([none3, low, none2], axis=0)
    slab[3] = jnp.concatenate([none3, high, none2], axis=0)
    t64 = tg[...]
    t128 = jnp.concatenate([t64, t64], axis=1)
    t256 = jnp.concatenate([t128, t128], axis=1)
    lane = lax.broadcasted_iota(jnp.int32, (8, BLK), 1)
    tgb[r] = jnp.where(lane // OWN == r, jnp.broadcast_to(t256, (8, BLK)), 0)

    pl.semaphore_wait(barrier, len(peers))

    zc = [
        send(slab.at[j], zb.at[j], zs.at[j], zrs.at[j], dev(x, y, zpeer(off), c))
        for j, off in ((1, -sg), (2, 2 * sg), (3, -3 * sg))
    ]
    mates = [dev(x, y, z, 1 - c), dev(x, y, zn, c), dev(x, y, zn, 1 - c)]
    mate_r = [lax.rem(r + 1, 2) + 2 * (r // 2), lax.rem(r + 2, 4), 3 - r]
    tc = [send(tgb.at[r], tgb.at[r], tss.at[k], trs.at[k], mates[k]) for k in range(3)]
    uc = [send(ub.at[own_rows, :], ub.at[own_rows, :], uss.at[k], urs.at[k], mates[k]) for k in range(3)]

    loads[3].wait()
    for l in range(LEVELS):
        cbt[:, l * K : (l + 1) * K] = cb[l * K : (l + 1) * K, :].astype(F32).T.astype(BF16)
    iota_k[...] = lax.broadcasted_iota(jnp.int32, (K, LANES), 0).astype(F32).astype(BF16)
    n = lax.broadcasted_iota(jnp.int32, (ITEMS // LANES, LANES), 0)
    k = lax.broadcasted_iota(jnp.int32, (ITEMS // LANES, LANES), 1)
    zj = (z - sg * (2 * (n % 2) + k // OWN) + NZ) % NZ
    uj = ((x + n // 16) % NX) * NY + (y + (n // 2) % NY) % NY
    col[...] = (zj * 2 + c) * 2048 + uj * OWN + k % OWN

    for cp in zc:
        cp.wait()
    yb[0] = (slab[0] + zb[1]) + (zb[2] + zb[3])
    yc = [send(yb.at[0], yb.at[NY - d], yss.at[d], yrs.at[d], dev(x, ypeer(d), z, c)) for d in range(1, NY)]
    for cp in tc + uc:
        cp.wait()
    us[...] = (ub[...].astype(F32) * (D**-0.5)).astype(BF16)
    tsum = (tgb[0] + tgb[1]) + (tgb[2] + tgb[3])
    tcol[...] = jnp.broadcast_to(tsum[0:1].astype(F32), (LANES, BLK)).T.astype(jnp.int32)
    mrun[...] = jnp.full((BLK, LANES), -1e30, F32)
    srun[...] = jnp.zeros((BLK, LANES), F32)
    pos[...] = jnp.zeros((BLK, LANES), F32)
    wacc[...] = jnp.zeros((K, BLK), F32)
    for cp in yc:
        cp.wait()
    xb[0] = yb[...].reshape(NY * 8, LANES).astype(BF16)
    xc = [send(xb.at[0], xb.at[NX - d], xss.at[d], xrs.at[d], dev(xpeer(d), y, z, c)) for d in range(1, NX)]

    def score(j, carry):
        base = pl.multiple_of(j * CHUNK, CHUNK)
        rows = xb[j // 2, pl.ds(pl.multiple_of(lax.rem(j, 2) * 32, 32), 32), :].astype(F32)
        for b in range(SUBS):
            for l in range(LEVELS):
                at = (b // 2) * 8 + (b % 2) * 3 + l
                row = jnp.broadcast_to(rows[at : at + 1, :], (16, LANES)).astype(BF16)
                hit = iota_k[...].reshape(K // 16, 16, LANES) == row[None]
                one = jnp.where(hit, jnp.ones((), BF16), jnp.zeros((), BF16))
                oh[l * K : (l + 1) * K, pl.ds(base + b * LANES, LANES)] = one.reshape(K, LANES)
        here = pl.ds(base, CHUNK)
        v = dot(cbt[...], oh[:, here]).astype(BF16)
        vt[:, here] = v
        lgt = dot(us[...], v)
        lg[:, here] = lgt
        m_old = mrun[...]
        m_new = m_old
        for b in range(SUBS):
            m_new = jnp.maximum(m_new, lgt[:, b * LANES : (b + 1) * LANES])
        s = srun[...] * jnp.exp(m_old - m_new)
        for b in range(SUBS):
            s = s + jnp.exp(lgt[:, b * LANES : (b + 1) * LANES] - m_new)
        mrun[...] = m_new
        srun[...] = s
        return carry

    lax.fori_loop(0, STEPS // NX, score, 0)
    for cp in xc:
        cp.wait()
    lax.fori_loop(STEPS // NX, STEPS, score, 0)

    mt = mrun[...].T
    st = srun[...].T
    m1 = jnp.max(mt, axis=0, keepdims=True)
    s1 = jnp.sum(st * jnp.exp(mt - m1), axis=0, keepdims=True)
    first = lax.broadcasted_iota(jnp.int32, (8, BLK), 0) == 0
    stat[r] = jnp.where(first, jnp.broadcast_to(m1, (8, BLK)), jnp.broadcast_to(s1, (8, BLK)))
    sc = [send(stat.at[r], stat.at[r], sss.at[k], srs.at[k], mates[k]) for k in range(3)]
    for cp in sc:
        cp.wait()
    ms = [stat[k][0:1] for k in range(GROUP)]
    top = jnp.maximum(jnp.maximum(ms[0], ms[1]), jnp.maximum(ms[2], ms[3]))
    tot = [stat[k][1:2] * jnp.exp(ms[k] - top) for k in range(GROUP)]
    lse = top + jnp.log((tot[0] + tot[1]) + (tot[2] + tot[3]))
    lsec[...] = jnp.broadcast_to(lse, (LANES, BLK)).T

    def grads(j, carry):
        base = pl.multiple_of(j * CHUNK, CHUNK)
        cols = col[pl.ds(pl.multiple_of(j * SUBS, SUBS), SUBS), :]
        for b in range(SUBS):
            here = pl.ds(base + b * LANES, LANES)
            lgt = lg[:, here]
            hit = tcol[...] == cols[b : b + 1, :]
            p = jnp.exp(lgt - lsec[...]) - jnp.where(hit, 1.0, 0.0)
            pos[...] += jnp.where(hit, lgt, 0.0)
            dl[:, here] = p.astype(BF16)
        here = pl.ds(base, CHUNK)
        wacc[...] += dot_t(oh[0:K, here], dl[:, here])
        return carry

    lax.fori_loop(0, STEPS, grads, 0)

    def level_out(l, w):
        hi = w.astype(BF16)
        rest = w - hi.astype(F32)
        mid = rest.astype(BF16)
        lo = (rest - mid.astype(F32)).astype(BF16)
        ubv = ub[...]
        out = (dot(hi, ubv) + dot(mid, ubv) + dot(lo, ubv)) * (D**-0.5)
        cbuf[l, 0] = out[:, :LANES]
        cbuf[l, 1] = out[:, LANES:]
        return send(cbuf.at[l, 1 - c], dbuf.at[l], ds.at[l], dr.at[l], dev(x, y, z, 1 - c))

    xrows = pl.ds(pl.multiple_of(x * 64, 64), 64)
    yrows = pl.ds(pl.multiple_of(y * 8, 8), 8)

    def x_send(l, cp):
        cp.wait()
        part[l] = cbuf[l, c] + dbuf[l]
        xr[l, x] = part[l, xrows, :]
        return [
            send(
                part.at[l, pl.ds(pl.multiple_of(xpeer(d) * 64, 64), 64), :], xr.at[l, x],
                xs1.at[l, d], xr1.at[l, d], dev(xpeer(d), y, z, c),
            )
            for d in range(1, NX)
        ]

    def l_send(val, buf, at, ss, rs, peer, count):
        buf[at] = val
        return [send(buf.at[at], buf.at[at], ss.at[d], rs.at[d], peer(d)) for d in range(1, count)]

    d0 = level_out(0, wacc[...])
    loss_part = 0.25 * jnp.sum(lse) - jnp.sum(pos[...])
    lv[...] = jnp.full((8, LANES), loss_part, F32)
    ldc = l_send(lv[...], ld, c, lds, ldr, lambda d: dev(x, y, z, 1 - c), 2)
    d1 = level_out(1, dot_t(oh[K : 2 * K, :], dl[...]))
    x0 = x_send(0, d0)
    for cp in ldc:
        cp.wait()
    lxc = l_send(ld[0] + ld[1], lx, x, lxs, lxr, lambda d: dev(xpeer(d), y, z, c), NX)
    d2 = level_out(2, dot_t(oh[2 * K : 3 * K, :], dl[...]))
    x1 = x_send(1, d1)
    gus[...] = dot_t(dl[...], vt[...]) * (D**-0.5)
    x2 = x_send(2, d2)
    guc = [
        send(
            gus.at[pl.ds(pl.multiple_of(mate_r[k] * OWN, OWN), OWN), :], gur.at[r],
            gss.at[k], grs.at[k], mates[k],
        )
        for k in range(3)
    ]
    gur[r] = gus[own_rows, :]

    def y_send(l, cps):
        for cp in cps:
            cp.wait()
        s = (xr[l, 0] + xr[l, 1]) + (xr[l, 2] + xr[l, 3])
        ys[l] = s
        yr[l, y] = ys[l, yrows, :]
        return [
            send(
                ys.at[l, pl.ds(pl.multiple_of(ypeer(d) * 8, 8), 8), :], yr.at[l, y],
                ys1.at[l, d], yr1.at[l, d], dev(x, ypeer(d), z, c),
            )
            for d in range(1, NY)
        ]

    def sum8(ref):
        return ((ref[0] + ref[1]) + (ref[2] + ref[3])) + ((ref[4] + ref[5]) + (ref[6] + ref[7]))

    def z_send(l, cps):
        for cp in cps:
            cp.wait()
        zr[l, z] = sum8(yr.at[l])
        return [
            send(zr.at[l, z], zr.at[l, z], zs1.at[l, d], zr1.at[l, d], dev(x, y, zpeer(d), c))
            for d in range(1, NZ)
        ]

    def y_back(l, cps):
        for cp in cps:
            cp.wait()
        ay[l, yrows, :] = sum8(zr.at[l])
        return [
            send(ay.at[l, yrows, :], ay.at[l, yrows, :], ys2.at[l, d], yr2.at[l, d], dev(x, ypeer(d), z, c))
            for d in range(1, NY)
        ]

    def x_back(l, cps):
        for cp in cps:
            cp.wait()
        fin[c, l, xrows, :] = ay[l]
        return [
            send(
                fin.at[c, l, xrows, :], fin.at[c, l, xrows, :],
                xs2.at[l, d], xr2.at[l, d], dev(xpeer(d), y, z, c),
            )
            for d in range(1, NX)
        ]

    def core_back(l, cps):
        for cp in cps:
            cp.wait()
        return send(fin.at[c, l], fin.at[c, l], ds2.at[l], dr2.at[l], dev(x, y, z, 1 - c))

    y0 = y_send(0, x0)
    for cp in lxc:
        cp.wait()
    lyc = l_send(
        (lx[0] + lx[1]) + (lx[2] + lx[3]), ly, y, lys, lyr, lambda d: dev(x, ypeer(d), z, c), NY
    )
    y1 = y_send(1, x1)
    y2 = y_send(2, x2)
    for cp in guc:
        cp.wait()
    gu_ref[...] = (gur[0] + gur[1]) + (gur[2] + gur[3])
    z0 = z_send(0, y0)
    for cp in lyc:
        cp.wait()
    lzc = l_send(sum8(ly), lz, z, lzs, lzr, lambda d: dev(x, y, zpeer(d), c), NZ)
    z1 = z_send(1, y1)
    z2 = z_send(2, y2)
    b0 = y_back(0, z0)
    for cp in lzc:
        cp.wait()
    loss_ref[...] = sum8(lz)[0:1, 0:1] * (1.0 / USERS)
    b1 = y_back(1, z1)
    b2 = y_back(2, z2)
    a0 = x_back(0, b0)
    a1 = x_back(1, b1)
    a2 = x_back(2, b2)
    e0 = core_back(0, a0)
    e1 = core_back(1, a1)
    e2 = core_back(2, a2)
    for l, cp in enumerate((e0, e1, e2)):
        cp.wait()
        gc_ref[l, :, 0:LANES] = fin[0, l]
        gc_ref[l, :, LANES:] = fin[1, l]


def shards(user_emb, item_codes, targets, codebook):
    vmem = pltpu.VMEM
    dma = pltpu.SemaphoreType.DMA
    scratch = [
        vmem((BLK, D), BF16), vmem((BLK, D), BF16), vmem((LEVELS, OWN), jnp.int32), vmem((1, OWN), jnp.int32),
        vmem((4, 8, LANES), F32), vmem((4, 8, LANES), F32), vmem((NY, 8, LANES), F32),
        vmem((NX, NY * 8, LANES), BF16), vmem((GROUP, 8, BLK), jnp.int32),
        vmem((LEVELS * K, D), BF16), vmem((D, LEVELS * K), BF16), vmem((K, LANES), BF16),
        vmem((ITEMS // LANES, LANES), jnp.int32),
        vmem((LEVELS * K, ITEMS), BF16), vmem((D, ITEMS), BF16), vmem((BLK, ITEMS), F32), vmem((BLK, ITEMS), BF16),
        vmem((BLK, LANES), F32), vmem((BLK, LANES), F32), vmem((GROUP, 8, BLK), F32), vmem((BLK, LANES), F32),
        vmem((BLK, LANES), jnp.int32), vmem((BLK, LANES), F32),
        vmem((K, BLK), F32), vmem((LEVELS, 2, K, LANES), F32), vmem((LEVELS, K, LANES), F32),
        vmem((LEVELS, K, LANES), F32), vmem((LEVELS, NX, 64, LANES), F32), vmem((LEVELS, 64, LANES), F32),
        vmem((LEVELS, NY, 8, LANES), F32), vmem((LEVELS, NZ, 8, LANES), F32), vmem((LEVELS, 64, LANES), F32),
        vmem((2, LEVELS, K, LANES), F32),
        vmem((BLK, D), F32), vmem((GROUP, OWN, D), F32), vmem((8, LANES), F32), vmem((2, 8, LANES), F32),
        vmem((NX, 8, LANES), F32), vmem((NY, 8, LANES), F32), vmem((NZ, 8, LANES), F32),
        dma((4,)), dma((4,)), dma((4,)), dma((3,)), dma((3,)), dma((3,)), dma((3,)),
        dma((NY,)), dma((NY,)), dma((NX,)), dma((NX,)), dma((3,)), dma((3,)),
        dma((LEVELS,)), dma((LEVELS,)), dma((LEVELS, NX)), dma((LEVELS, NX)), dma((LEVELS, NY)), dma((LEVELS, NY)),
        dma((LEVELS, NZ)), dma((LEVELS, NZ)), dma((LEVELS, NY)), dma((LEVELS, NY)), dma((LEVELS, NX)), dma((LEVELS, NX)),
        dma((LEVELS,)), dma((LEVELS,)), dma((3,)), dma((3,)),
        dma((2,)), dma((2,)), dma((NX,)), dma((NX,)), dma((NY,)), dma((NY,)), dma((NZ,)), dma((NZ,)),
    ]
    gu, gc, loss = pl.pallas_call(
        kernel,
        out_shape=(
            jax.ShapeDtypeStruct((OWN, D), F32),
            jax.ShapeDtypeStruct((LEVELS, K, D), F32),
            jax.ShapeDtypeStruct((1, 1), F32),
        ),
        in_specs=[pl.BlockSpec(memory_space=pl.ANY)] * 4,
        out_specs=[pl.BlockSpec(memory_space=vmem)] * 3,
        scratch_shapes=scratch,
        compiler_params=pltpu.CompilerParams(
            collective_id=0, has_side_effects=True, vmem_limit_bytes=56 * 2**20
        ),
        cost_estimate=pl.CostEstimate(flops=9 * 10**9, bytes_accessed=2 * 10**6, transcendentals=4 * 10**6),
    )(user_emb, item_codes, targets.reshape(1, OWN), codebook.reshape(LEVELS * K, D))
    return gu, gc, loss.reshape(())


def solution(mesh):
    return jax.shard_map(
        shards,
        mesh=mesh,
        in_specs=(P(("user", "item"), None), P(None, ("item", "user")), P(("user", "item")), P()),
        out_specs=(P(("user", "item"), None), P(), P()),
        check_vma=False,
    )
```

time: 735 us -> 88.3 us (0.12)
  waiting for transfers between devices: 484 us -> 0 us
  blocking collectives: 193 us -> 0 us
  Pallas kernels: 0 us -> 82.1 us
  matrix products: 19.3 us -> 0 us
  between operations: 16.4 us -> 2.39 us
  other arithmetic: 13.4 us -> 0 us
    psum x1 -> x0, waiting for transfers between devices: 233 us -> none  [shards(): lax.psum((cb_terms, jnp.sum(row_losses)), ('user', 'item'))]
    reduce_scatter x2 -> x0, waiting for transfers between devices: 209 us -> none  [the longest x1 209 us: shards(): lax.psum_scatter(lax.dot_general(dlogits, block_users, (((0,), (0,)), (()...]
    psum x2 -> x0, blocking collectives: 127 us -> none  [the longest x1 103 us: shards(): lax.psum((cb_terms, jnp.sum(row_losses)), ('user', 'item'))]
    pallas_call x0 -> x1, Pallas kernels: none -> 82.1 us  [shards(): pl.pallas_call(kernel, out_shape=(jax.ShapeDtypeStruct((OWN, D), F32), ja...]
    all_gather x1 -> x0, waiting for transfers between devices: 42.3 us -> none  [shards(): block_items = lax.all_gather(own_vectors, 'user', axis=0, tiled=True)]
    pmax x1 -> x0, blocking collectives: 29 us -> none  [shards(): row_max = lax.pmax(local_max, 'item')]
    all_gather x1 -> x0, blocking collectives: 19.6 us -> none  [shards(): lax.all_gather(user_emb, 'item', axis=0, tiled=True)]
    dot_general x15 -> x0, matrix products: 19.3 us -> none  [the longest x1 5.73 us: shards(): lax.dot_general(block_users, block_items, (((1,), (1,)), ((), ())), prefe...]
  transfers between devices with their start and end apart: 4 -> 0, of which waited for: 3 -> 0; matrix products, arithmetic and copies ran while one was open for 2% -> 0% of each run, Pallas kernels for 0% -> 0%
where the time goes in v1:
time: 88.3 us; the launch traced here: 88.1 us
  Pallas kernels  82.1 us (93%)
  local copies, waits for them, and re-layouts  3.54 us (4%)
  between operations  2.39 us (3%)
    pallas_call x1, Pallas kernels, shards(): pl.pallas_call(kernel, out_shape=(jax.ShapeDtypeStruct((OWN, D), F32), ja...  82.1 us
    unnamed x2, local copies, waits for them, and re-layouts  3.54 us

profile of v1, /device:TPU:1, one launch (start us, length us, event | category | flops | bytes accessed | tf_op | source)
XLA Modules:
  0.0 88.1 jit_solution(13128813264421347632)
XLA Ops:
  0.6 82.1 %shard_map.67 = (f32[64,256]{1,0:T(8,128)}, f32[3,256,256]{2,1,0:T(8,128)}, f32[1,1]{1,0:T(1,128)}) custom-call(bf16[64,256]{1,0:T(8,128)(2,1)} %ue_hbm.1, s32[3,64]{1,0:T(4,128)} %codes_hbm.1, s32[1,64]{1,0:T(1,128)} %bitcast.4, bf16[768,256]{1,0:T(8,128)(2,1)} %bitcast.3), custom_call_target="tpu_custom_call" | custom-call | flops 8999999488 | bytes 2000000 | tf_op jit(solution)/shard_map/pallas_call | solution.py:371
  82.8 1.5 %copy.10 = f32[64,256]{1,0:T(8,128)} copy(f32[64,256]{1,0:T(8,128)} %get-tuple-element.12) | data formatting | bytes 131072
  84.2 2.1 %copy.11 = f32[3,256,256]{2,1,0:T(8,128)} copy(f32[3,256,256]{2,1,0:T(8,128)} %get-tuple-element.13) | data formatting | bytes 1572864

commit v2 on v1

v2 whole, which is shorter than its diff:
```python
import jax
import jax.numpy as jnp
from jax import lax
from jax.experimental import pallas as pl
from jax.experimental.pallas import tpu as pltpu
from jax.sharding import PartitionSpec as P

MESH = pl.DeviceIdType.MESH
NX, NY, NZ = 4, 8, 8
D = 256
K = 256
LEVELS = 3
OWN = 64
GROUP = 4
BLK = GROUP * OWN
ITEMS = 8192
CHUNK = 1024
STEPS = ITEMS // CHUNK
LANES = 128
SUBS = CHUNK // LANES
ROWS = 32
USERS = 32768
FAR = {4: (2, 1, 3), 8: (4, 3, 5, 2, 6, 1, 7)}
F32 = jnp.float32
BF16 = jnp.bfloat16


def dot(a, b):
    return jnp.dot(a, b, preferred_element_type=F32)


def dot_t(a, b):
    return lax.dot_general(a, b, (((1,), (1,)), ((), ())), preferred_element_type=F32)


def kernel(
    ue_hbm, codes_hbm, tg_hbm, cb_hbm, gu_ref, gc_ref, loss_ref,
    ub, us, cd, tg, slab, zb, yb, xb, tgb, cb, cbt, iota_k, col,
    oh, vt, lg, dl, mrun, srun, stat, lsec, tcol, pos,
    cbuf, dbuf, part, r1, s2, r2, r3, a4, fin,
    gus, gur, ld, lx, ly, lz,
    loc, zs, zrs, tss, trs, uss, urs, yss, yrs, xss, xrs, sss, srs,
    ds, dr, s1s, s1r, s2s, s2r, s3s, s3r, s4s, s4r, s5s, s5r, ds2, dr2, gss, grs,
    lds, ldr, lxs, lxr, lys, lyr, lzs, lzr,
):
    u, i = lax.axis_index("user"), lax.axis_index("item")
    x, y = u // NY, lax.rem(u, NY)
    z, c = i // 2, lax.rem(i, 2)
    r = lax.rem(i, GROUP)
    sg = 1 - 2 * lax.rem(z, 2)

    def dev(x_, y_, z_, c_):
        return (x_ * NY + y_, z_ * 2 + c_)

    def xpeer(d):
        return lax.rem(x + d, NX)

    def ypeer(d):
        return lax.rem(y + d, NY)

    def zpeer(d):
        return lax.rem(z + d + NZ, NZ)

    zn = z + sg

    barrier = pltpu.get_barrier_semaphore()
    peers = [dev(xpeer(d), y, z, c) for d in range(1, NX)]
    peers += [dev(x, ypeer(d), z, c) for d in range(1, NY)]
    peers += [dev(x, y, zpeer(d), c) for d in range(1, NZ)]
    peers += [dev(x, y, z, 1 - c), dev(x, y, zn, 1 - c)]
    for peer in peers:
        pl.semaphore_signal(barrier, inc=1, device_id=peer, device_id_type=MESH)

    sent = []

    def send(src, dst, ss, rs, to):
        copy = pltpu.make_async_remote_copy(
            src_ref=src, dst_ref=dst, send_sem=ss, recv_sem=rs, device_id=to, device_id_type=MESH
        )
        copy.start()
        sent.append(copy)
        return copy

    own_rows = pl.ds(pl.multiple_of(r * OWN, OWN), OWN)
    loads = [
        pltpu.make_async_copy(codes_hbm, cd, loc.at[0]),
        pltpu.make_async_copy(tg_hbm, tg, loc.at[1]),
        pltpu.make_async_copy(ue_hbm, ub.at[own_rows, :], loc.at[2]),
        pltpu.make_async_copy(cb_hbm, cb, loc.at[3]),
    ]
    for load in loads:
        load.start()
    for load in loads[:3]:
        load.wait()

    own = cd[...].astype(F32)
    low = jnp.concatenate([own, jnp.zeros((LEVELS, OWN), F32)], axis=1)
    high = jnp.concatenate([jnp.zeros((LEVELS, OWN), F32), own], axis=1)
    none3 = jnp.zeros((3, LANES), F32)
    none2 = jnp.zeros((2, LANES), F32)
    slab[0] = jnp.concatenate([low, none3, none2], axis=0)
    slab[1] = jnp.concatenate([high, none3, none2], axis=0)
    slab[2] = jnp.concatenate([none3, low, none2], axis=0)
    slab[3] = jnp.concatenate([none3, high, none2], axis=0)
    t64 = tg[...]
    t128 = jnp.concatenate([t64, t64], axis=1)
    t256 = jnp.concatenate([t128, t128], axis=1)
    lane = lax.broadcasted_iota(jnp.int32, (8, BLK), 1)
    tgb[r] = jnp.where(lane // OWN == r, jnp.broadcast_to(t256, (8, BLK)), 0)

    pl.semaphore_wait(barrier, len(peers))

    zc = [
        send(slab.at[j], zb.at[j], zs.at[j], zrs.at[j], dev(x, y, zpeer(off), c))
        for j, off in ((3, -3 * sg), (2, 2 * sg), (1, -sg))
    ]
    mates = [dev(x, y, z, 1 - c), dev(x, y, zn, c), dev(x, y, zn, 1 - c)]
    mate_r = [lax.rem(r + 1, 2) + 2 * (r // 2), lax.rem(r + 2, 4), 3 - r]
    tc = [send(tgb.at[r], tgb.at[r], tss.at[k], trs.at[k], mates[k]) for k in range(3)]
    uc = [send(ub.at[own_rows, :], ub.at[own_rows, :], uss.at[k], urs.at[k], mates[k]) for k in range(3)]

    loads[3].wait()
    for l in range(LEVELS):
        cbt[:, l * K : (l + 1) * K] = cb[l * K : (l + 1) * K, :].astype(F32).T.astype(BF16)
    iota_k[...] = lax.broadcasted_iota(jnp.int32, (K, LANES), 0).astype(F32).astype(BF16)
    n = lax.broadcasted_iota(jnp.int32, (ITEMS // LANES, LANES), 0)
    k = lax.broadcasted_iota(jnp.int32, (ITEMS // LANES, LANES), 1)
    zj = (z - sg * (2 * (n % 2) + k // OWN) + NZ) % NZ
    uj = ((x + n // 16) % NX) * NY + (y + (n // 2) % NY) % NY
    col[...] = (zj * 2 + c) * 2048 + uj * OWN + k % OWN

    for cp in zc:
        cp.wait_recv()
    yb[0] = (slab[0] + zb[1]) + (zb[2] + zb[3])
    yc = [send(yb.at[0], yb.at[NY - d], yss.at[d], yrs.at[d], dev(x, ypeer(d), z, c)) for d in FAR[NY]]
    for cp in tc + uc:
        cp.wait_recv()
    us[...] = (ub[...].astype(F32) * (D**-0.5)).astype(BF16)
    tsum = (tgb[0] + tgb[1]) + (tgb[2] + tgb[3])
    tcol[...] = jnp.broadcast_to(tsum[0:1].astype(F32), (LANES, BLK)).T.astype(jnp.int32)
    mrun[...] = jnp.full((BLK, LANES), -1e30, F32)
    srun[...] = jnp.zeros((BLK, LANES), F32)
    pos[...] = jnp.zeros((BLK, LANES), F32)
    for cp in yc:
        cp.wait_recv()
    xb[0] = yb[...].reshape(NY * 8, LANES).astype(BF16)
    xc = [send(xb.at[0], xb.at[NX - d], xss.at[d], xrs.at[d], dev(xpeer(d), y, z, c)) for d in FAR[NX]]

    def onehots(j):
        rows = xb[j // 2, (j % 2) * 32 : (j % 2) * 32 + 32, :].astype(F32)
        for b in range(SUBS):
            lanes = slice(j * CHUNK + b * LANES, j * CHUNK + (b + 1) * LANES)
            for l in range(LEVELS):
                at = (b // 2) * 8 + (b % 2) * 3 + l
                row = jnp.broadcast_to(rows[at : at + 1, :], (16, LANES)).astype(BF16)
                hit = iota_k[...].reshape(K // 16, 16, LANES) == row[None]
                one = jnp.where(hit, jnp.ones((), BF16), jnp.zeros((), BF16))
                oh[l * K : (l + 1) * K, lanes] = one.reshape(K, LANES)

    def span(j):
        return slice(j * CHUNK, (j + 1) * CHUNK)

    def stats(j):
        for top in range(0, BLK, ROWS):
            rows = slice(top, top + ROWS)
            tiles = [slice(j * CHUNK + b * LANES, j * CHUNK + (b + 1) * LANES) for b in range(SUBS)]
            m_old = mrun[rows]
            m_new = m_old
            for t in tiles:
                m_new = jnp.maximum(m_new, lg[rows, t])
            s = srun[rows] * jnp.exp(m_old - m_new)
            for t in tiles:
                s = s + jnp.exp(lg[rows, t] - m_new)
            mrun[rows] = m_new
            srun[rows] = s

    def score(first, last):
        onehots(first)
        for j in range(first, last + 2):
            if j < last:
                vt[:, span(j)] = dot(cbt[...], oh[:, span(j)]).astype(BF16)
            if j + 1 < last:
                onehots(j + 1)
            if first <= j - 1 < last:
                lg[:, span(j - 1)] = dot(us[...], vt[:, span(j - 1)])
            if first <= j - 2:
                stats(j - 2)

    score(0, STEPS // NX)
    for cp in xc:
        cp.wait_recv()
    score(STEPS // NX, STEPS)

    mt = mrun[...].T
    st = srun[...].T
    m1 = jnp.max(mt, axis=0, keepdims=True)
    s1 = jnp.sum(st * jnp.exp(mt - m1), axis=0, keepdims=True)
    first = lax.broadcasted_iota(jnp.int32, (8, BLK), 0) == 0
    stat[r] = jnp.where(first, jnp.broadcast_to(m1, (8, BLK)), jnp.broadcast_to(s1, (8, BLK)))
    sc = [send(stat.at[r], stat.at[r], sss.at[k], srs.at[k], mates[k]) for k in range(3)]
    for cp in sc:
        cp.wait_recv()
    ms = [stat[k][0:1] for k in range(GROUP)]
    top = jnp.maximum(jnp.maximum(ms[0], ms[1]), jnp.maximum(ms[2], ms[3]))
    tot = [stat[k][1:2] * jnp.exp(ms[k] - top) for k in range(GROUP)]
    lse = top + jnp.log((tot[0] + tot[1]) + (tot[2] + tot[3]))
    lsec[...] = jnp.broadcast_to(lse, (LANES, BLK)).T

    def dlogits(j):
        for top in range(0, BLK, ROWS):
            rows = slice(top, top + ROWS)
            t, e, found = tcol[rows], lsec[rows], pos[rows]
            for b in range(SUBS):
                lanes = slice(j * CHUNK + b * LANES, j * CHUNK + (b + 1) * LANES)
                v = lg[rows, lanes]
                hit = t == col[j * SUBS + b : j * SUBS + b + 1, :]
                p = jnp.exp(v - e)
                found = jnp.where(hit, v, found)
                dl[rows, lanes] = jnp.where(hit, p - 1.0, p).astype(BF16)
            pos[rows] = found

    dlogits(0)
    w = jnp.zeros((LEVELS * K, BLK), F32)
    for j in range(STEPS):
        w = w + dot_t(oh[:, span(j)], dl[:, span(j)])
        if j + 1 < STEPS:
            dlogits(j + 1)

    def level_out(l, w):
        hi = w.astype(BF16)
        rest = w - hi.astype(F32)
        mid = rest.astype(BF16)
        lo = (rest - mid.astype(F32)).astype(BF16)
        ubv = ub[...]
        out = (dot(hi, ubv) + dot(mid, ubv) + dot(lo, ubv)) * (D**-0.5)
        cbuf[l, 0] = out[:, :LANES]
        cbuf[l, 1] = out[:, LANES:]
        return send(cbuf.at[l, 1 - c], dbuf.at[l], ds.at[l], dr.at[l], dev(x, y, z, 1 - c))

    size = {"x": NX, "y": NY, "z": NZ}
    here = {"x": x, "y": y, "z": z}

    def along(a, d):
        if a == "x":
            return dev(xpeer(d), y, z, c)
        if a == "y":
            return dev(x, ypeer(d), z, c)
        return dev(x, y, zpeer(d), c)

    def block(at, rows):
        return pl.ds(pl.multiple_of(at * rows, 8), rows)

    def done(copies):
        for cp in copies:
            cp.wait_recv()

    def scatter(l, a, src, into, rows, ss, rs):
        n = size[a]
        into[l, block(here[a], rows), :] = src[l, block(here[a], rows), :]
        return [
            send(
                src.at[l, block(lax.rem(here[a] + d, n), rows), :], into.at[l, block(here[a], rows), :],
                ss.at[l, d], rs.at[l, d], along(a, d),
            )
            for d in FAR[n]
        ]

    def spread(buf, pre, a, rows, ss, rs, sem):
        at = buf.at[pre + (block(here[a], rows), slice(None))]
        return [send(at, at, ss.at[sem + (d,)], rs.at[sem + (d,)], along(a, d)) for d in FAR[size[a]]]

    def total(buf, pre, a, rows):
        parts = [buf[pre + (slice(k * rows, (k + 1) * rows), slice(None))] for k in range(size[a])]
        while len(parts) > 1:
            parts = [p + q for p, q in zip(parts[::2], parts[1::2])]
        return parts[0]

    ways = (("y", "x", "z"), ("z", "x", "y"), ("x", "y", "z"))

    def first(l, cp):
        cp.wait_recv()
        part[l] = cbuf[l, c] + dbuf[l]
        return scatter(l, ways[l][0], part, r1, K // size[ways[l][0]], s1s, s1r)

    def second(l, copies):
        done(copies)
        a, b, _ = ways[l]
        rows = K // size[a]
        s2[l, 0:rows, :] = total(r1, (l,), a, rows)
        return scatter(l, b, s2, r2, 8, s2s, s2r)

    def third(l, copies):
        done(copies)
        _, b, e = ways[l]
        r3[l, block(here[e], 8), :] = total(r2, (l,), b, 8)
        return spread(r3, (l,), e, 8, s3s, s3r, (l,))

    def fourth(l, copies):
        done(copies)
        _, b, e = ways[l]
        a4[l, block(here[b], 8), :] = total(r3, (l,), e, 8)
        return spread(a4, (l,), b, 8, s4s, s4r, (l,))

    def fifth(l, copies):
        done(copies)
        a = ways[l][0]
        rows = K // size[a]
        fin[c, l, block(here[a], rows), :] = a4[l, 0:rows, :]
        return spread(fin, (c, l), a, rows, s5s, s5r, (l,))

    def pass_on(l, at, rows, sem):
        there = fin.at[c, l, block(at, rows), :]
        return send(there, there, ds2.at[l, sem], dr2.at[l, sem], dev(x, y, z, 1 - c))

    def last(l, copies):
        a = ways[l][0]
        n = size[a]
        rows = K // n
        out = [pass_on(l, here[a], rows, 0)]
        for d, cp in sorted(zip(FAR[n], copies), key=lambda t: min(t[0], n - t[0])):
            cp.wait_recv()
            out.append(pass_on(l, lax.rem(here[a] + n - d, n), rows, d))
        return out

    def loss_over(a, val, buf, ss, rs):
        buf[block(here[a], 8), :] = val
        return spread(buf, (), a, 8, ss, rs, ())

    d0 = level_out(0, w[0:K])
    loss_part = 0.25 * jnp.sum(lse) - jnp.sum(pos[...])
    ld[c] = jnp.full((8, LANES), loss_part, F32)
    ldc = send(ld.at[c], ld.at[c], lds.at[0], ldr.at[0], dev(x, y, z, 1 - c))
    d1 = level_out(1, w[K : 2 * K])
    f0 = first(0, d0)
    d2 = level_out(2, w[2 * K :])
    f1 = first(1, d1)
    ldc.wait_recv()
    lxc = loss_over("x", ld[0] + ld[1], lx, lxs, lxr)
    gus[...] = dot_t(dl[...], vt[...]) * (D**-0.5)
    f2 = first(2, d2)
    g0 = second(0, f0)
    g1 = second(1, f1)
    done(lxc)
    lyc = loss_over("y", total(lx, (), "x", 8), ly, lys, lyr)
    g2 = second(2, f2)
    guc = [
        send(gus.at[block(mate_r[k], OWN), :], gur.at[r], gss.at[k], grs.at[k], mates[k]) for k in range(3)
    ]
    gur[r] = gus[own_rows, :]
    h0 = third(0, g0)
    h1 = third(1, g1)
    h2 = third(2, g2)
    done(lyc)
    lzc = loss_over("z", total(ly, (), "y", 8), lz, lzs, lzr)
    j0 = fourth(0, h0)
    j1 = fourth(1, h1)
    j2 = fourth(2, h2)
    done(lzc)
    loss_ref[...] = total(lz, (), "z", 8)[0:1, 0:1] * (1.0 / USERS)
    done(guc)
    gu_ref[...] = (gur[0] + gur[1]) + (gur[2] + gur[3])
    k0 = fifth(0, j0)
    k1 = fifth(1, j1)
    k2 = fifth(2, j2)
    e2 = last(2, k2)
    e0 = last(0, k0)
    e1 = last(1, k1)
    for l, copies in ((2, e2), (0, e0), (1, e1)):
        done(copies)
        gc_ref[l, :, 0:LANES] = fin[0, l]
        gc_ref[l, :, LANES:] = fin[1, l]
    for cp in sent:
        cp.wait_send()


def hand_over(gu_in, gc_in, loss_in, gu_ref, gc_ref, loss_ref):
    gu_ref[...] = gu_in[...]
    gc_ref[...] = gc_in[...]
    loss_ref[...] = loss_in[...]


def shards(user_emb, item_codes, targets, codebook):
    vmem = pltpu.VMEM
    dma = pltpu.SemaphoreType.DMA
    scratch = [
        vmem((BLK, D), BF16), vmem((BLK, D), BF16), vmem((LEVELS, OWN), jnp.int32), vmem((1, OWN), jnp.int32),
        vmem((4, 8, LANES), F32), vmem((4, 8, LANES), F32), vmem((NY, 8, LANES), F32),
        vmem((NX, NY * 8, LANES), BF16), vmem((GROUP, 8, BLK), jnp.int32),
        vmem((LEVELS * K, D), BF16), vmem((D, LEVELS * K), BF16), vmem((K, LANES), BF16),
        vmem((ITEMS // LANES, LANES), jnp.int32),
        vmem((LEVELS * K, ITEMS), BF16), vmem((D, ITEMS), BF16), vmem((BLK, ITEMS), F32), vmem((BLK, ITEMS), BF16),
        vmem((BLK, LANES), F32), vmem((BLK, LANES), F32), vmem((GROUP, 8, BLK), F32), vmem((BLK, LANES), F32),
        vmem((BLK, LANES), jnp.int32), vmem((BLK, LANES), F32),
        vmem((LEVELS, 2, K, LANES), F32), vmem((LEVELS, K, LANES), F32), vmem((LEVELS, K, LANES), F32),
        vmem((LEVELS, K, LANES), F32), vmem((LEVELS, 64, LANES), F32), vmem((LEVELS, 64, LANES), F32),
        vmem((LEVELS, 64, LANES), F32), vmem((LEVELS, 64, LANES), F32), vmem((2, LEVELS, K, LANES), F32),
        vmem((BLK, D), F32), vmem((GROUP, OWN, D), F32), vmem((2, 8, LANES), F32),
        vmem((NX * 8, LANES), F32), vmem((NY * 8, LANES), F32), vmem((NZ * 8, LANES), F32),
        dma((4,)), dma((4,)), dma((4,)), dma((3,)), dma((3,)), dma((3,)), dma((3,)),
        dma((NY,)), dma((NY,)), dma((NX,)), dma((NX,)), dma((3,)), dma((3,)),
        dma((LEVELS,)), dma((LEVELS,)), *[dma((LEVELS, 8)) for _ in range(10)],
        dma((LEVELS, 8)), dma((LEVELS, 8)), dma((3,)), dma((3,)),
        dma((2,)), dma((2,)), dma((NX,)), dma((NX,)), dma((NY,)), dma((NY,)), dma((NZ,)), dma((NZ,)),
    ]
    gu, gc, loss = pl.pallas_call(
        kernel,
        out_shape=(
            jax.ShapeDtypeStruct((OWN, D), F32),
            jax.ShapeDtypeStruct((LEVELS, K, D), F32),
            jax.ShapeDtypeStruct((1, 1), F32),
        ),
        in_specs=[pl.BlockSpec(memory_space=pl.ANY)] * 4,
        out_specs=[pl.BlockSpec(memory_space=vmem)] * 3,
        scratch_shapes=scratch,
        compiler_params=pltpu.CompilerParams(
            collective_id=0, has_side_effects=True, vmem_limit_bytes=56 * 2**20
        ),
        cost_estimate=pl.CostEstimate(flops=9 * 10**9, bytes_accessed=2 * 10**6, transcendentals=4 * 10**6),
    )(user_emb, item_codes, targets.reshape(1, OWN), codebook.reshape(LEVELS * K, D))
    gu, gc, loss = pl.pallas_call(
        hand_over,
        out_shape=tuple(jax.ShapeDtypeStruct(a.shape, F32) for a in (gu, gc, loss)),
        in_specs=[pl.BlockSpec(memory_space=vmem)] * 3,
        out_specs=[pl.BlockSpec(memory_space=vmem)] * 3,
    )(gu, gc, loss)
    return gu, gc, loss.reshape(())


def solution(mesh):
    return jax.shard_map(
        shards,
        mesh=mesh,
        in_specs=(P(("user", "item"), None), P(None, ("item", "user")), P(("user", "item")), P()),
        out_specs=(P(("user", "item"), None), P(), P()),
        check_vma=False,
    )
```

time: 88.3 us -> 77.2 us (0.87)
  Pallas kernels: 82.1 us -> 76.4 us
  local copies, waits for them, and re-layouts: 3.54 us -> 0 us
  between operations: 2.39 us -> 0.64 us
    pallas_call x1, Pallas kernels: 82.1 us -> 73.7 us  [shards(): pl.pallas_call(kernel, out_shape=(jax.ShapeDtypeStruct((OWN, D), F32), ja...]
    unnamed x2 -> x0, local copies, waits for them, and re-layouts: 3.54 us -> none
    pallas_call x0 -> x1, Pallas kernels: none -> 2.67 us  [shards(): pl.pallas_call(hand_over, out_shape=tuple((jax.ShapeDtypeStruct(a.shape,...]
where the time goes in v2:
time: 77.2 us; the launch traced here: 77 us
  Pallas kernels  76.4 us (99%)
    pallas_call x1, Pallas kernels, shards(): pl.pallas_call(kernel, out_shape=(jax.ShapeDtypeStruct((OWN, D), F32), ja...  73.7 us
    pallas_call x1, Pallas kernels, shards(): pl.pallas_call(hand_over, out_shape=tuple((jax.ShapeDtypeStruct(a.shape,...  2.67 us

profile of v2, /device:TPU:1, one launch (start us, length us, event | category | flops | bytes accessed | tf_op | source)
XLA Modules:
  0.0 77.0 jit_solution(2037342413124114161)
XLA Ops:
  0.6 73.7 %shard_map.67 = (f32[64,256]{1,0:T(8,128)}, f32[3,256,256]{2,1,0:T(8,128)}, f32[1,1]{1,0:T(1,128)}) custom-call(bf16[64,256]{1,0:T(8,128)(2,1)} %ue_hbm.1, s32[3,64]{1,0:T(4,128)} %codes_hbm.1, s32[1,64]{1,0:T(1,128)} %bitcast.4, bf16[768,256]{1,0:T(8,128)(2,1)} %bitcast.3), custom_call_target="tpu_custom_call" | custom-call | flops 8999999488 | bytes 2000000 | tf_op jit(solution)/shard_map/pallas_call | solution.py:405
  74.4 2.7 %shard_map.68 = (f32[64,256]{1,0:T(8,128)}, f32[3,256,256]{2,1,0:T(8,128)}, f32[1,1]{1,0:T(1,128)}) custom-call(f32[64,256]{1,0:T(8,128)} %get-tuple-element.9.gu_in, f32[3,256,256]{2,1,0:T(8,128)} %get-tuple-element.10.gc_in, f32[1,1]{1,0:T(1,128)} %get-tuple-element.11.loss_in), custom_call_target="tpu_custom_call" | custom-call | tf_op jit(solution)/shard_map/pallas_call | solution.py:420

commit v3 on v2

--- a/solution.py
+++ b/solution.py
@@ -11,15 +11,16 @@
 K = 256
 LEVELS = 3
 OWN = 64
-GROUP = 4
+GROUP = 8
 BLK = GROUP * OWN
-ITEMS = 8192
+ITEMS = 4096
 CHUNK = 1024
 STEPS = ITEMS // CHUNK
 LANES = 128
 SUBS = CHUNK // LANES
 ROWS = 32
 USERS = 32768
+SLOT = (0, 1, 7, 2, 6, 3, 5, 4)
 FAR = {4: (2, 1, 3), 8: (4, 3, 5, 2, 6, 1, 7)}
 F32 = jnp.float32
 BF16 = jnp.bfloat16
@@ -35,19 +36,18 @@
 
 def kernel(
     ue_hbm, codes_hbm, tg_hbm, cb_hbm, gu_ref, gc_ref, loss_ref,
-    ub, us, cd, tg, slab, zb, yb, xb, tgb, cb, cbt, iota_k, col,
+    ub, us, cd, tg, slab, zb, yb, tgb, cb, cbt, iota_k, col,
     oh, vt, lg, dl, mrun, srun, stat, lsec, tcol, pos,
     cbuf, dbuf, part, r1, s2, r2, r3, a4, fin,
-    gus, gur, ld, lx, ly, lz,
-    loc, zs, zrs, tss, trs, uss, urs, yss, yrs, xss, xrs, sss, srs,
-    ds, dr, s1s, s1r, s2s, s2r, s3s, s3r, s4s, s4r, s5s, s5r, ds2, dr2, gss, grs,
+    gus, gud, gup, gur, guo, ld, lx, ly, lz,
+    loc, zs, zrs, tss, trs, uss, urs, yss, yrs, sss, srs,
+    ds, dr, s1s, s1r, s2s, s2r, s3s, s3r, s4s, s4r, s5s, s5r, ds2, dr2, gds, gdr, gss, grs, oss,
     lds, ldr, lxs, lxr, lys, lyr, lzs, lzr,
 ):
     u, i = lax.axis_index("user"), lax.axis_index("item")
     x, y = u // NY, lax.rem(u, NY)
     z, c = i // 2, lax.rem(i, 2)
-    r = lax.rem(i, GROUP)
-    sg = 1 - 2 * lax.rem(z, 2)
+    r = x * 2 + c
 
     def dev(x_, y_, z_, c_):
         return (x_ * NY + y_, z_ * 2 + c_)
@@ -61,13 +61,11 @@
     def zpeer(d):
         return lax.rem(z + d + NZ, NZ)
 
-    zn = z + sg
-
     barrier = pltpu.get_barrier_semaphore()
-    peers = [dev(xpeer(d), y, z, c) for d in range(1, NX)]
-    peers += [dev(x, ypeer(d), z, c) for d in range(1, NY)]
-    peers += [dev(x, y, zpeer(d), c) for d in range(1, NZ)]
-    peers += [dev(x, y, z, 1 - c), dev(x, y, zn, 1 - c)]
+    peers = [dev(x, y, zpeer(d), c) for d in FAR[NZ]]
+    peers += [dev(x, ypeer(d), z, c) for d in FAR[NY]]
+    mates = [dev(xpeer(d), y, z, e) for d in FAR[NX] for e in (c, 1 - c)] + [dev(x, y, z, 1 - c)]
+    peers += mates
     for peer in peers:
         pl.semaphore_signal(barrier, inc=1, device_id=peer, device_id_type=MESH)
 
@@ -102,22 +100,22 @@
     slab[1] = jnp.concatenate([high, none3, none2], axis=0)
     slab[2] = jnp.concatenate([none3, low, none2], axis=0)
     slab[3] = jnp.concatenate([none3, high, none2], axis=0)
-    t64 = tg[...]
-    t128 = jnp.concatenate([t64, t64], axis=1)
-    t256 = jnp.concatenate([t128, t128], axis=1)
-    lane = lax.broadcasted_iota(jnp.int32, (8, BLK), 1)
-    tgb[r] = jnp.where(lane // OWN == r, jnp.broadcast_to(t256, (8, BLK)), 0)
+    t128 = jnp.concatenate([tg[...], tg[...]], axis=1)
+    row8 = lax.broadcasted_iota(jnp.int32, (8, LANES), 0)
+    lane = lax.broadcasted_iota(jnp.int32, (8, LANES), 1)
+    mine = (row8 == x) & (lane // OWN == c)
+    tgb[r] = jnp.where(mine, jnp.broadcast_to(t128, (8, LANES)), 0)
 
     pl.semaphore_wait(barrier, len(peers))
 
+    zb[0] = slab[0]
     zc = [
-        send(slab.at[j], zb.at[j], zs.at[j], zrs.at[j], dev(x, y, zpeer(off), c))
-        for j, off in ((3, -3 * sg), (2, 2 * sg), (1, -sg))
+        send(slab.at[(NZ - d) % 4], zb.at[NZ - d], zs.at[d], zrs.at[d], dev(x, y, zpeer(d), c)) for d in FAR[NZ]
     ]
-    mates = [dev(x, y, z, 1 - c), dev(x, y, zn, c), dev(x, y, zn, 1 - c)]
-    mate_r = [lax.rem(r + 1, 2) + 2 * (r // 2), lax.rem(r + 2, 4), 3 - r]
-    tc = [send(tgb.at[r], tgb.at[r], tss.at[k], trs.at[k], mates[k]) for k in range(3)]
-    uc = [send(ub.at[own_rows, :], ub.at[own_rows, :], uss.at[k], urs.at[k], mates[k]) for k in range(3)]
+    tc = [send(tgb.at[r], tgb.at[r], tss.at[k], trs.at[k], mates[k]) for k in range(GROUP - 1)]
+    uc = [
+        send(ub.at[own_rows, :], ub.at[own_rows, :], uss.at[k], urs.at[k], mates[k]) for k in range(GROUP - 1)
+    ]
 
     loads[3].wait()
     for l in range(LEVELS):
@@ -125,34 +123,39 @@
     iota_k[...] = lax.broadcasted_iota(jnp.int32, (K, LANES), 0).astype(F32).astype(BF16)
     n = lax.broadcasted_iota(jnp.int32, (ITEMS // LANES, LANES), 0)
     k = lax.broadcasted_iota(jnp.int32, (ITEMS // LANES, LANES), 1)
-    zj = (z - sg * (2 * (n % 2) + k // OWN) + NZ) % NZ
-    uj = ((x + n // 16) % NX) * NY + (y + (n // 2) % NY) % NY
-    col[...] = (zj * 2 + c) * 2048 + uj * OWN + k % OWN
+    step = n // 4
+    dy = jnp.where(step % 2 == 1, (step + 1) // 2, (NY - step // 2) % NY)
+    zj = (z + 2 * (n % 4) + k // OWN) % NZ
+    col[...] = (zj * 2 + c) * 2048 + (x * NY + (y + dy) % NY) * OWN + k % OWN
 
     for cp in zc:
         cp.wait_recv()
-    yb[0] = (slab[0] + zb[1]) + (zb[2] + zb[3])
-    yc = [send(yb.at[0], yb.at[NY - d], yss.at[d], yrs.at[d], dev(x, ypeer(d), z, c)) for d in FAR[NY]]
+    halves = [(zb[k] + zb[k + 1]) + (zb[k + 2] + zb[k + 3]) for k in (0, 4)]
+    yb[0] = jnp.concatenate(halves, axis=0).astype(BF16)
+    yc = {
+        NY - d: send(yb.at[0], yb.at[SLOT.index(NY - d)], yss.at[d], yrs.at[d], dev(x, ypeer(d), z, c))
+        for d in FAR[NY]
+    }
     for cp in tc + uc:
         cp.wait_recv()
     us[...] = (ub[...].astype(F32) * (D**-0.5)).astype(BF16)
-    tsum = (tgb[0] + tgb[1]) + (tgb[2] + tgb[3])
-    tcol[...] = jnp.broadcast_to(tsum[0:1].astype(F32), (LANES, BLK)).T.astype(jnp.int32)
+    tsum = ((tgb[0] + tgb[1]) + (tgb[2] + tgb[3])) + ((tgb[4] + tgb[5]) + (tgb[6] + tgb[7]))
+
+    def column(row):
+        return jnp.broadcast_to(row, (LANES, LANES)).T
+
+    for q in range(BLK // LANES):
+        tcol[q * LANES : (q + 1) * LANES, :] = column(tsum[q : q + 1].astype(F32)).astype(jnp.int32)
     mrun[...] = jnp.full((BLK, LANES), -1e30, F32)
     srun[...] = jnp.zeros((BLK, LANES), F32)
     pos[...] = jnp.zeros((BLK, LANES), F32)
-    for cp in yc:
-        cp.wait_recv()
-    xb[0] = yb[...].reshape(NY * 8, LANES).astype(BF16)
-    xc = [send(xb.at[0], xb.at[NX - d], xss.at[d], xrs.at[d], dev(xpeer(d), y, z, c)) for d in FAR[NX]]
-
     def onehots(j):
-        rows = xb[j // 2, (j % 2) * 32 : (j % 2) * 32 + 32, :].astype(F32)
+        rows = [yb[2 * j].astype(F32), yb[2 * j + 1].astype(F32)]
         for b in range(SUBS):
             lanes = slice(j * CHUNK + b * LANES, j * CHUNK + (b + 1) * LANES)
             for l in range(LEVELS):
-                at = (b // 2) * 8 + (b % 2) * 3 + l
-                row = jnp.broadcast_to(rows[at : at + 1, :], (16, LANES)).astype(BF16)
+                at = (b % 4 // 2) * 8 + (b % 2) * 3 + l
+                row = jnp.broadcast_to(rows[b // 4][at : at + 1, :], (16, LANES)).astype(BF16)
                 hit = iota_k[...].reshape(K // 16, 16, LANES) == row[None]
                 one = jnp.where(hit, jnp.ones((), BF16), jnp.zeros((), BF16))
                 oh[l * K : (l + 1) * K, lanes] = one.reshape(K, LANES)
@@ -186,26 +189,29 @@
             if first <= j - 2:
                 stats(j - 2)
 
-    score(0, STEPS // NX)
-    for cp in xc:
-        cp.wait_recv()
-    score(STEPS // NX, STEPS)
+    for first in (0, STEPS // 2):
+        for at in range(max(1, 2 * first), 2 * first + STEPS):
+            yc[SLOT[at]].wait_recv()
+        score(first, first + STEPS // 2)
 
     mt = mrun[...].T
     st = srun[...].T
     m1 = jnp.max(mt, axis=0, keepdims=True)
     s1 = jnp.sum(st * jnp.exp(mt - m1), axis=0, keepdims=True)
-    first = lax.broadcasted_iota(jnp.int32, (8, BLK), 0) == 0
-    stat[r] = jnp.where(first, jnp.broadcast_to(m1, (8, BLK)), jnp.broadcast_to(s1, (8, BLK)))
-    sc = [send(stat.at[r], stat.at[r], sss.at[k], srs.at[k], mates[k]) for k in range(3)]
+    quarters = [slice(q * LANES, (q + 1) * LANES) for q in range(BLK // LANES)]
+    stat[r] = jnp.concatenate([m1[:, q] for q in quarters] + [s1[:, q] for q in quarters], axis=0)
+    sc = [send(stat.at[r], stat.at[r], sss.at[k], srs.at[k], mates[k]) for k in range(GROUP - 1)]
     for cp in sc:
         cp.wait_recv()
-    ms = [stat[k][0:1] for k in range(GROUP)]
-    top = jnp.maximum(jnp.maximum(ms[0], ms[1]), jnp.maximum(ms[2], ms[3]))
-    tot = [stat[k][1:2] * jnp.exp(ms[k] - top) for k in range(GROUP)]
-    lse = top + jnp.log((tot[0] + tot[1]) + (tot[2] + tot[3]))
-    lsec[...] = jnp.broadcast_to(lse, (LANES, BLK)).T
-
+    ms = [stat[k][0:4] for k in range(GROUP)]
+    top = ms[0]
+    for k in range(1, GROUP):
+        top = jnp.maximum(top, ms[k])
+    tot = [stat[k][4:8] * jnp.exp(ms[k] - top) for k in range(GROUP)]
+    tot = ((tot[0] + tot[1]) + (tot[2] + tot[3])) + ((tot[4] + tot[5]) + (tot[6] + tot[7]))
+    lse = top + jnp.log(tot)
+    for q in range(BLK // LANES):
+        lsec[q * LANES : (q + 1) * LANES, :] = column(lse[q : q + 1])
     def dlogits(j):
         for top in range(0, BLK, ROWS):
             rows = slice(top, top + ROWS)
@@ -327,7 +333,7 @@
         return spread(buf, (), a, 8, ss, rs, ())
 
     d0 = level_out(0, w[0:K])
-    loss_part = 0.25 * jnp.sum(lse) - jnp.sum(pos[...])
+    loss_part = (1.0 / GROUP) * jnp.sum(lse) - jnp.sum(pos[...])
     ld[c] = jnp.full((8, LANES), loss_part, F32)
     ldc = send(ld.at[c], ld.at[c], lds.at[0], ldr.at[0], dev(x, y, z, 1 - c))
     d1 = level_out(1, w[K : 2 * K])
@@ -336,29 +342,36 @@
     f1 = first(1, d1)
     ldc.wait_recv()
     lxc = loss_over("x", ld[0] + ld[1], lx, lxs, lxr)
-    gus[...] = dot_t(dl[...], vt[...]) * (D**-0.5)
+    gu = dot_t(dl[...], vt[...]) * (D**-0.5)
+    for k in range(GROUP):
+        gus[k // 2, k % 2] = gu[k * OWN : (k + 1) * OWN]
+    gdc = send(gus.at[:, 1 - c], gud, gds.at[0], gdr.at[0], dev(x, y, z, 1 - c))
     f2 = first(2, d2)
     g0 = second(0, f0)
     g1 = second(1, f1)
     done(lxc)
     lyc = loss_over("y", total(lx, (), "x", 8), ly, lys, lyr)
     g2 = second(2, f2)
-    guc = [
-        send(gus.at[block(mate_r[k], OWN), :], gur.at[r], gss.at[k], grs.at[k], mates[k]) for k in range(3)
-    ]
-    gur[r] = gus[own_rows, :]
     h0 = third(0, g0)
     h1 = third(1, g1)
     h2 = third(2, g2)
     done(lyc)
     lzc = loss_over("z", total(ly, (), "y", 8), lz, lzs, lzr)
+    gdc.wait_recv()
+    gup[...] = gus[:, c] + gud[...]
+    gur[x] = gup[x]
+    guc = [
+        send(gup.at[xpeer(d)], gur.at[x], gss.at[d], grs.at[d], dev(xpeer(d), y, z, c)) for d in FAR[NX]
+    ]
     j0 = fourth(0, h0)
     j1 = fourth(1, h1)
     j2 = fourth(2, h2)
     done(lzc)
     loss_ref[...] = total(lz, (), "z", 8)[0:1, 0:1] * (1.0 / USERS)
     done(guc)
-    gu_ref[...] = (gur[0] + gur[1]) + (gur[2] + gur[3])
+    guo[...] = (gur[0] + gur[1]) + (gur[2] + gur[3])
+    outs = [pltpu.make_async_copy(guo, gu_ref, oss.at[0, 0])]
+    outs[0].start()
     k0 = fifth(0, j0)
     k1 = fifth(1, j1)
     k2 = fifth(2, j2)
@@ -367,16 +380,30 @@
     e1 = last(1, k1)
     for l, copies in ((2, e2), (0, e0), (1, e1)):
         done(copies)
-        gc_ref[l, :, 0:LANES] = fin[0, l]
-        gc_ref[l, :, LANES:] = fin[1, l]
+        for half in range(2):
+            out = pltpu.make_async_copy(
+                fin.at[half, l], gc_ref.at[l, :, half * LANES : (half + 1) * LANES], oss.at[half, l + 1]
+            )
+            out.start()
+            outs.append(out)
+    for out in outs:
+        out.wait()
     for cp in sent:
         cp.wait_send()
 
 
-def hand_over(gu_in, gc_in, loss_in, gu_ref, gc_ref, loss_ref):
-    gu_ref[...] = gu_in[...]
-    gc_ref[...] = gc_in[...]
+def hand_over(gu_in, gc_in, loss_in, gu_ref, gc_ref, loss_ref, gu, gc, ins, outs):
+    pieces = [(gu_in, gu, gu_ref)] + [(gc_in.at[l], gc.at[l], gc_ref.at[l]) for l in range(LEVELS)]
+    loads = [pltpu.make_async_copy(p[0], p[1], ins.at[k]) for k, p in enumerate(pieces)]
+    stores = [pltpu.make_async_copy(p[1], p[2], outs.at[k]) for k, p in enumerate(pieces)]
+    for load in loads:
+        load.start()
     loss_ref[...] = loss_in[...]
+    for load, store in zip(loads, stores):
+        load.wait()
+        store.start()
+    for store in stores:
+        store.wait()
 
 
 def shards(user_emb, item_codes, targets, codebook):
@@ -384,22 +411,23 @@
     dma = pltpu.SemaphoreType.DMA
     scratch = [
         vmem((BLK, D), BF16), vmem((BLK, D), BF16), vmem((LEVELS, OWN), jnp.int32), vmem((1, OWN), jnp.int32),
-        vmem((4, 8, LANES), F32), vmem((4, 8, LANES), F32), vmem((NY, 8, LANES), F32),
-        vmem((NX, NY * 8, LANES), BF16), vmem((GROUP, 8, BLK), jnp.int32),
+        vmem((4, 8, LANES), F32), vmem((NZ, 8, LANES), F32), vmem((NY, 16, LANES), BF16),
+        vmem((GROUP, 8, LANES), jnp.int32),
         vmem((LEVELS * K, D), BF16), vmem((D, LEVELS * K), BF16), vmem((K, LANES), BF16),
         vmem((ITEMS // LANES, LANES), jnp.int32),
         vmem((LEVELS * K, ITEMS), BF16), vmem((D, ITEMS), BF16), vmem((BLK, ITEMS), F32), vmem((BLK, ITEMS), BF16),
-        vmem((BLK, LANES), F32), vmem((BLK, LANES), F32), vmem((GROUP, 8, BLK), F32), vmem((BLK, LANES), F32),
+        vmem((BLK, LANES), F32), vmem((BLK, LANES), F32), vmem((GROUP, 8, LANES), F32), vmem((BLK, LANES), F32),
         vmem((BLK, LANES), jnp.int32), vmem((BLK, LANES), F32),
         vmem((LEVELS, 2, K, LANES), F32), vmem((LEVELS, K, LANES), F32), vmem((LEVELS, K, LANES), F32),
         vmem((LEVELS, K, LANES), F32), vmem((LEVELS, 64, LANES), F32), vmem((LEVELS, 64, LANES), F32),
         vmem((LEVELS, 64, LANES), F32), vmem((LEVELS, 64, LANES), F32), vmem((2, LEVELS, K, LANES), F32),
-        vmem((BLK, D), F32), vmem((GROUP, OWN, D), F32), vmem((2, 8, LANES), F32),
+        vmem((NX, 2, OWN, D), F32), vmem((NX, OWN, D), F32), vmem((NX, OWN, D), F32), vmem((NX, OWN, D), F32),
+        vmem((OWN, D), F32), vmem((2, 8, LANES), F32),
         vmem((NX * 8, LANES), F32), vmem((NY * 8, LANES), F32), vmem((NZ * 8, LANES), F32),
-        dma((4,)), dma((4,)), dma((4,)), dma((3,)), dma((3,)), dma((3,)), dma((3,)),
-        dma((NY,)), dma((NY,)), dma((NX,)), dma((NX,)), dma((3,)), dma((3,)),
+        dma((4,)), dma((NZ,)), dma((NZ,)), dma((GROUP,)), dma((GROUP,)), dma((GROUP,)), dma((GROUP,)),
+        dma((NY,)), dma((NY,)), dma((GROUP,)), dma((GROUP,)),
         dma((LEVELS,)), dma((LEVELS,)), *[dma((LEVELS, 8)) for _ in range(10)],
-        dma((LEVELS, 8)), dma((LEVELS, 8)), dma((3,)), dma((3,)),
+        dma((LEVELS, 8)), dma((LEVELS, 8)), dma((1,)), dma((1,)), dma((NX,)), dma((NX,)), dma((2, LEVELS + 1)),
         dma((2,)), dma((2,)), dma((NX,)), dma((NX,)), dma((NY,)), dma((NY,)), dma((NZ,)), dma((NZ,)),
     ]
     gu, gc, loss = pl.pallas_call(
@@ -410,7 +438,7 @@
             jax.ShapeDtypeStruct((1, 1), F32),
         ),
         in_specs=[pl.BlockSpec(memory_space=pl.ANY)] * 4,
-        out_specs=[pl.BlockSpec(memory_space=vmem)] * 3,
+        out_specs=[pl.BlockSpec(memory_space=m) for m in (pl.ANY, pl.ANY, vmem)],
         scratch_shapes=scratch,
         compiler_params=pltpu.CompilerParams(
             collective_id=0, has_side_effects=True, vmem_limit_bytes=56 * 2**20
@@ -420,8 +448,9 @@
     gu, gc, loss = pl.pallas_call(
         hand_over,
         out_shape=tuple(jax.ShapeDtypeStruct(a.shape, F32) for a in (gu, gc, loss)),
-        in_specs=[pl.BlockSpec(memory_space=vmem)] * 3,
-        out_specs=[pl.BlockSpec(memory_space=vmem)] * 3,
+        in_specs=[pl.BlockSpec(memory_space=m) for m in (pl.ANY, pl.ANY, vmem)],
+        out_specs=[pl.BlockSpec(memory_space=m) for m in (pl.ANY, pl.ANY, vmem)],
+        scratch_shapes=[vmem((OWN, D), F32), vmem((LEVELS, K, D), F32), dma((4,)), dma((4,))],
     )(gu, gc, loss)
     return gu, gc, loss.reshape(())
 

time: 77.2 us -> 73.3 us (0.949)
  Pallas kernels: 76.4 us -> 72.5 us
    pallas_call x1, Pallas kernels: 73.7 us -> 69.5 us  [shards(): pl.pallas_call(kernel, out_shape=(jax.ShapeDtypeStruct((OWN, D), F32), ja...]
where the time goes in v3:
time: 73.3 us; the launch traced here: 73.1 us
  Pallas kernels  72.5 us (99%)
    pallas_call x1, Pallas kernels, shards(): pl.pallas_call(kernel, out_shape=(jax.ShapeDtypeStruct((OWN, D), F32), ja...  69.5 us
    pallas_call x1, Pallas kernels, shards(): pl.pallas_call(hand_over, out_shape=tuple((jax.ShapeDtypeStruct(a.shape,...  3 us

profile of v3, /device:TPU:1, one launch (start us, length us, event | category | flops | bytes accessed | tf_op | source)
XLA Modules:
  0.0 73.1 jit_solution(4257966625879078421)
XLA Ops:
  0.6 69.5 %shard_map.67 = (f32[64,256]{1,0:T(8,128)}, f32[3,256,256]{2,1,0:T(8,128)}, f32[1,1]{1,0:T(1,128)}) custom-call(bf16[64,256]{1,0:T(8,128)(2,1)} %ue_hbm.1, s32[3,64]{1,0:T(4,128)} %codes_hbm.1, s32[1,64]{1,0:T(1,128)} %bitcast.4, bf16[768,256]{1,0:T(8,128)(2,1)} %bitcast.3), custom_call_target="tpu_custom_call" | custom-call | flops 8999999488 | bytes 2000000 | tf_op jit(solution)/shard_map/pallas_call | solution.py:433
  70.1 3.0 %shard_map.68 = (f32[64,256]{1,0:T(8,128)}, f32[3,256,256]{2,1,0:T(8,128)}, f32[1,1]{1,0:T(1,128)}) custom-call(f32[64,256]{1,0:T(8,128)} %get-tuple-element.9.gu_in, f32[3,256,256]{2,1,0:T(8,128)} %get-tuple-element.10.gc_in, f32[1,1]{1,0:T(1,128)} %get-tuple-element.11.loss_in), custom_call_target="tpu_custom_call" | custom-call | tf_op jit(solution)/shard_map/pallas_call | solution.py:448

commit v4 on v3

--- a/solution.py
+++ b/solution.py
@@ -14,10 +14,11 @@
 GROUP = 8
 BLK = GROUP * OWN
 ITEMS = 4096
-CHUNK = 1024
-STEPS = ITEMS // CHUNK
 LANES = 128
-SUBS = CHUNK // LANES
+SUBS = ITEMS // LANES
+SCORE = (0, 4, 8, 16, 24, 32)
+HALF = 16
+GRADS = (0, 8, 16, 24, 32)
 ROWS = 32
 USERS = 32768
 SLOT = (0, 1, 7, 2, 6, 3, 5, 4)
@@ -39,9 +40,9 @@
     ub, us, cd, tg, slab, zb, yb, tgb, cb, cbt, iota_k, col,
     oh, vt, lg, dl, mrun, srun, stat, lsec, tcol, pos,
     cbuf, dbuf, part, r1, s2, r2, r3, a4, fin,
-    gus, gud, gup, gur, guo, ld, lx, ly, lz,
+    gus, gud, gup, gur, ld, lx, ly, lz,
     loc, zs, zrs, tss, trs, uss, urs, yss, yrs, sss, srs,
-    ds, dr, s1s, s1r, s2s, s2r, s3s, s3r, s4s, s4r, s5s, s5r, ds2, dr2, gds, gdr, gss, grs, oss,
+    ds, dr, s1s, s1r, s2s, s2r, s3s, s3r, s4s, s4r, s5s, s5r, ds2, dr2, gds, gdr, gss, grs,
     lds, ldr, lxs, lxr, lys, lyr, lzs, lzr,
 ):
     u, i = lax.axis_index("user"), lax.axis_index("item")
@@ -149,50 +150,54 @@
     mrun[...] = jnp.full((BLK, LANES), -1e30, F32)
     srun[...] = jnp.zeros((BLK, LANES), F32)
     pos[...] = jnp.zeros((BLK, LANES), F32)
+    def tile(b):
+        return slice(b * LANES, (b + 1) * LANES)
+
+    def span(steps, j):
+        return slice(steps[j] * LANES, steps[j + 1] * LANES)
+
     def onehots(j):
-        rows = [yb[2 * j].astype(F32), yb[2 * j + 1].astype(F32)]
-        for b in range(SUBS):
-            lanes = slice(j * CHUNK + b * LANES, j * CHUNK + (b + 1) * LANES)
+        for b in range(SCORE[j], SCORE[j + 1]):
+            rows = yb[b // 4].astype(F32)
             for l in range(LEVELS):
                 at = (b % 4 // 2) * 8 + (b % 2) * 3 + l
-                row = jnp.broadcast_to(rows[b // 4][at : at + 1, :], (16, LANES)).astype(BF16)
+                row = jnp.broadcast_to(rows[at : at + 1, :], (16, LANES)).astype(BF16)
                 hit = iota_k[...].reshape(K // 16, 16, LANES) == row[None]
                 one = jnp.where(hit, jnp.ones((), BF16), jnp.zeros((), BF16))
-                oh[l * K : (l + 1) * K, lanes] = one.reshape(K, LANES)
-
-    def span(j):
-        return slice(j * CHUNK, (j + 1) * CHUNK)
+                oh[l * K : (l + 1) * K, tile(b)] = one.reshape(K, LANES)
 
     def stats(j):
+        blocks = range(SCORE[j], SCORE[j + 1])
         for top in range(0, BLK, ROWS):
             rows = slice(top, top + ROWS)
-            tiles = [slice(j * CHUNK + b * LANES, j * CHUNK + (b + 1) * LANES) for b in range(SUBS)]
             m_old = mrun[rows]
             m_new = m_old
-            for t in tiles:
-                m_new = jnp.maximum(m_new, lg[rows, t])
+            for b in blocks:
+                m_new = jnp.maximum(m_new, lg[rows, tile(b)])
             s = srun[rows] * jnp.exp(m_old - m_new)
-            for t in tiles:
-                s = s + jnp.exp(lg[rows, t] - m_new)
+            for b in blocks:
+                s = s + jnp.exp(lg[rows, tile(b)] - m_new)
             mrun[rows] = m_new
             srun[rows] = s
 
-    def score(first, last):
-        onehots(first)
-        for j in range(first, last + 2):
-            if j < last:
-                vt[:, span(j)] = dot(cbt[...], oh[:, span(j)]).astype(BF16)
-            if j + 1 < last:
-                onehots(j + 1)
-            if first <= j - 1 < last:
-                lg[:, span(j - 1)] = dot(us[...], vt[:, span(j - 1)])
-            if first <= j - 2:
-                stats(j - 2)
-
-    for first in (0, STEPS // 2):
-        for at in range(max(1, 2 * first), 2 * first + STEPS):
+    def arrived(first, last):
+        for at in range(first, last):
             yc[SLOT[at]].wait_recv()
-        score(first, first + STEPS // 2)
+
+    steps = len(SCORE) - 1
+    arrived(1, HALF // 4)
+    onehots(0)
+    for j in range(steps + 2):
+        if j < steps:
+            vt[:, span(SCORE, j)] = dot(cbt[...], oh[:, span(SCORE, j)]).astype(BF16)
+        if j + 1 < steps:
+            if SCORE[j + 1] == HALF:
+                arrived(HALF // 4, NY)
+            onehots(j + 1)
+        if 1 <= j <= steps:
+            lg[:, span(SCORE, j - 1)] = dot(us[...], vt[:, span(SCORE, j - 1)])
+        if 2 <= j:
+            stats(j - 2)
 
     mt = mrun[...].T
     st = srun[...].T
@@ -216,20 +221,19 @@
         for top in range(0, BLK, ROWS):
             rows = slice(top, top + ROWS)
             t, e, found = tcol[rows], lsec[rows], pos[rows]
-            for b in range(SUBS):
-                lanes = slice(j * CHUNK + b * LANES, j * CHUNK + (b + 1) * LANES)
-                v = lg[rows, lanes]
-                hit = t == col[j * SUBS + b : j * SUBS + b + 1, :]
+            for b in range(GRADS[j], GRADS[j + 1]):
+                v = lg[rows, tile(b)]
+                hit = t == col[b : b + 1, :]
                 p = jnp.exp(v - e)
                 found = jnp.where(hit, v, found)
-                dl[rows, lanes] = jnp.where(hit, p - 1.0, p).astype(BF16)
+                dl[rows, tile(b)] = jnp.where(hit, p - 1.0, p).astype(BF16)
             pos[rows] = found
 
     dlogits(0)
     w = jnp.zeros((LEVELS * K, BLK), F32)
-    for j in range(STEPS):
-        w = w + dot_t(oh[:, span(j)], dl[:, span(j)])
-        if j + 1 < STEPS:
+    for j in range(len(GRADS) - 1):
+        w = w + dot_t(oh[:, span(GRADS, j)], dl[:, span(GRADS, j)])
+        if j + 2 < len(GRADS):
             dlogits(j + 1)
 
     def level_out(l, w):
@@ -333,8 +337,8 @@
         return spread(buf, (), a, 8, ss, rs, ())
 
     d0 = level_out(0, w[0:K])
-    loss_part = (1.0 / GROUP) * jnp.sum(lse) - jnp.sum(pos[...])
-    ld[c] = jnp.full((8, LANES), loss_part, F32)
+    own_lse = jnp.concatenate([lse * (1.0 / GROUP), jnp.zeros((4, LANES), F32)], axis=0)
+    ld[c] = own_lse - jnp.sum(pos[...].reshape(BLK // 8, 8, LANES), axis=0)
     ldc = send(ld.at[c], ld.at[c], lds.at[0], ldr.at[0], dev(x, y, z, 1 - c))
     d1 = level_out(1, w[K : 2 * K])
     f0 = first(0, d0)
@@ -342,11 +346,11 @@
     f1 = first(1, d1)
     ldc.wait_recv()
     lxc = loss_over("x", ld[0] + ld[1], lx, lxs, lxr)
+    f2 = first(2, d2)
     gu = dot_t(dl[...], vt[...]) * (D**-0.5)
     for k in range(GROUP):
         gus[k // 2, k % 2] = gu[k * OWN : (k + 1) * OWN]
     gdc = send(gus.at[:, 1 - c], gud, gds.at[0], gdr.at[0], dev(x, y, z, 1 - c))
-    f2 = first(2, d2)
     g0 = second(0, f0)
     g1 = second(1, f1)
     done(lxc)
@@ -367,11 +371,9 @@
     j1 = fourth(1, h1)
     j2 = fourth(2, h2)
     done(lzc)
-    loss_ref[...] = total(lz, (), "z", 8)[0:1, 0:1] * (1.0 / USERS)
+    loss_ref[...] = jnp.full((1, 1), jnp.sum(total(lz, (), "z", 8)) * (1.0 / USERS), F32)
     done(guc)
-    guo[...] = (gur[0] + gur[1]) + (gur[2] + gur[3])
-    outs = [pltpu.make_async_copy(guo, gu_ref, oss.at[0, 0])]
-    outs[0].start()
+    gu_ref[...] = (gur[0] + gur[1]) + (gur[2] + gur[3])
     k0 = fifth(0, j0)
     k1 = fifth(1, j1)
     k2 = fifth(2, j2)
@@ -380,30 +382,16 @@
     e1 = last(1, k1)
     for l, copies in ((2, e2), (0, e0), (1, e1)):
         done(copies)
-        for half in range(2):
-            out = pltpu.make_async_copy(
-                fin.at[half, l], gc_ref.at[l, :, half * LANES : (half + 1) * LANES], oss.at[half, l + 1]
-            )
-            out.start()
-            outs.append(out)
-    for out in outs:
-        out.wait()
+        gc_ref[l, :, :LANES] = fin[0, l]
+        gc_ref[l, :, LANES:] = fin[1, l]
     for cp in sent:
         cp.wait_send()
 
 
-def hand_over(gu_in, gc_in, loss_in, gu_ref, gc_ref, loss_ref, gu, gc, ins, outs):
-    pieces = [(gu_in, gu, gu_ref)] + [(gc_in.at[l], gc.at[l], gc_ref.at[l]) for l in range(LEVELS)]
-    loads = [pltpu.make_async_copy(p[0], p[1], ins.at[k]) for k, p in enumerate(pieces)]
-    stores = [pltpu.make_async_copy(p[1], p[2], outs.at[k]) for k, p in enumerate(pieces)]
-    for load in loads:
-        load.start()
+def hand_over(gu_in, gc_in, loss_in, gu_ref, gc_ref, loss_ref):
+    gu_ref[...] = gu_in[...]
+    gc_ref[...] = gc_in[...]
     loss_ref[...] = loss_in[...]
-    for load, store in zip(loads, stores):
-        load.wait()
-        store.start()
-    for store in stores:
-        store.wait()
 
 
 def shards(user_emb, item_codes, targets, codebook):
@@ -422,23 +410,19 @@
         vmem((LEVELS, K, LANES), F32), vmem((LEVELS, 64, LANES), F32), vmem((LEVELS, 64, LANES), F32),
         vmem((LEVELS, 64, LANES), F32), vmem((LEVELS, 64, LANES), F32), vmem((2, LEVELS, K, LANES), F32),
         vmem((NX, 2, OWN, D), F32), vmem((NX, OWN, D), F32), vmem((NX, OWN, D), F32), vmem((NX, OWN, D), F32),
-        vmem((OWN, D), F32), vmem((2, 8, LANES), F32),
+        vmem((2, 8, LANES), F32),
         vmem((NX * 8, LANES), F32), vmem((NY * 8, LANES), F32), vmem((NZ * 8, LANES), F32),
         dma((4,)), dma((NZ,)), dma((NZ,)), dma((GROUP,)), dma((GROUP,)), dma((GROUP,)), dma((GROUP,)),
         dma((NY,)), dma((NY,)), dma((GROUP,)), dma((GROUP,)),
         dma((LEVELS,)), dma((LEVELS,)), *[dma((LEVELS, 8)) for _ in range(10)],
-        dma((LEVELS, 8)), dma((LEVELS, 8)), dma((1,)), dma((1,)), dma((NX,)), dma((NX,)), dma((2, LEVELS + 1)),
+        dma((LEVELS, 8)), dma((LEVELS, 8)), dma((1,)), dma((1,)), dma((NX,)), dma((NX,)),
         dma((2,)), dma((2,)), dma((NX,)), dma((NX,)), dma((NY,)), dma((NY,)), dma((NZ,)), dma((NZ,)),
     ]
     gu, gc, loss = pl.pallas_call(
         kernel,
-        out_shape=(
-            jax.ShapeDtypeStruct((OWN, D), F32),
-            jax.ShapeDtypeStruct((LEVELS, K, D), F32),
-            jax.ShapeDtypeStruct((1, 1), F32),
-        ),
+        out_shape=tuple(jax.ShapeDtypeStruct(n, F32) for n in ((OWN, D), (LEVELS, K, D), (1, 1))),
         in_specs=[pl.BlockSpec(memory_space=pl.ANY)] * 4,
-        out_specs=[pl.BlockSpec(memory_space=m) for m in (pl.ANY, pl.ANY, vmem)],
+        out_specs=[pl.BlockSpec(memory_space=vmem)] * 3,
         scratch_shapes=scratch,
         compiler_params=pltpu.CompilerParams(
             collective_id=0, has_side_effects=True, vmem_limit_bytes=56 * 2**20
@@ -447,10 +431,9 @@
     )(user_emb, item_codes, targets.reshape(1, OWN), codebook.reshape(LEVELS * K, D))
     gu, gc, loss = pl.pallas_call(
         hand_over,
-        out_shape=tuple(jax.ShapeDtypeStruct(a.shape, F32) for a in (gu, gc, loss)),
-        in_specs=[pl.BlockSpec(memory_space=m) for m in (pl.ANY, pl.ANY, vmem)],
-        out_specs=[pl.BlockSpec(memory_space=m) for m in (pl.ANY, pl.ANY, vmem)],
-        scratch_shapes=[vmem((OWN, D), F32), vmem((LEVELS, K, D), F32), dma((4,)), dma((4,))],
+        out_shape=tuple(jax.ShapeDtypeStruct(n, F32) for n in ((OWN, D), (LEVELS, K, D), (1, 1))),
+        in_specs=[pl.BlockSpec(memory_space=vmem)] * 3,
+        out_specs=[pl.BlockSpec(memory_space=vmem)] * 3,
     )(gu, gc, loss)
     return gu, gc, loss.reshape(())
 

time: 73.3 us -> 72.6 us (level)
  no operation moved by 1% of the time
where the time goes in v4:
time: 72.6 us; the launch traced here: 72.4 us
  Pallas kernels  71.8 us (99%)
    pallas_call x1, Pallas kernels, shards(): pl.pallas_call(kernel, out_shape=tuple((jax.ShapeDtypeStruct(n, F32) for...  69.1 us
    pallas_call x1, Pallas kernels, shards(): pl.pallas_call(hand_over, out_shape=tuple((jax.ShapeDtypeStruct(n, F32) f...  2.67 us

profile of v4, /device:TPU:1, one launch (start us, length us, event | category | flops | bytes accessed | tf_op | source)
XLA Modules:
  0.0 72.4 jit_solution(2433950977520642747)
XLA Ops:
  0.6 69.1 %shard_map.67 = (f32[64,256]{1,0:T(8,128)}, f32[3,256,256]{2,1,0:T(8,128)}, f32[1,1]{1,0:T(1,128)}) custom-call(bf16[64,256]{1,0:T(8,128)(2,1)} %ue_hbm.1, s32[3,64]{1,0:T(4,128)} %codes_hbm.1, s32[1,64]{1,0:T(1,128)} %bitcast.4, bf16[768,256]{1,0:T(8,128)(2,1)} %bitcast.3), custom_call_target="tpu_custom_call" | custom-call | flops 8999999488 | bytes 2000000 | tf_op jit(solution)/shard_map/pallas_call | solution.py:421
  69.7 2.7 %shard_map.68 = (f32[64,256]{1,0:T(8,128)}, f32[3,256,256]{2,1,0:T(8,128)}, f32[1,1]{1,0:T(1,128)}) custom-call(f32[64,256]{1,0:T(8,128)} %get-tuple-element.9.gu_in, f32[3,256,256]{2,1,0:T(8,128)} %get-tuple-element.10.gc_in, f32[1,1]{1,0:T(1,128)} %get-tuple-element.11.loss_in), custom_call_target="tpu_custom_call" | custom-call | tf_op jit(solution)/shard_map/pallas_call | solution.py:432

commit v5 on v4

--- a/solution.py
+++ b/solution.py
@@ -41,8 +41,8 @@
     oh, vt, lg, dl, mrun, srun, stat, lsec, tcol, pos,
     cbuf, dbuf, part, r1, s2, r2, r3, a4, fin,
     gus, gud, gup, gur, ld, lx, ly, lz,
-    loc, zs, zrs, tss, trs, uss, urs, yss, yrs, sss, srs,
-    ds, dr, s1s, s1r, s2s, s2r, s3s, s3r, s4s, s4r, s5s, s5r, ds2, dr2, gds, gdr, gss, grs,
+    loc, zs, tss, uss, yss, sss,
+    ds, dr, s1s, s1r, s2s, s2r, s3s, s3r, s4s, s4r, s5s, s5r, ds2, dr2, gds, gdr, gss,
     lds, ldr, lxs, lxr, lys, lyr, lzs, lzr,
 ):
     u, i = lax.axis_index("user"), lax.axis_index("item")
@@ -72,13 +72,21 @@
 
     sent = []
 
+    def take(size, sem):
+        pltpu.make_async_copy(size, size, sem).wait()
+
+    def push(src, dst, ss, rs, to):
+        pltpu.make_async_remote_copy(
+            src_ref=src, dst_ref=dst, send_sem=ss, recv_sem=rs, device_id=to, device_id_type=MESH
+        ).start()
+
+    def pushed(size, ss, rs):
+        sent.append((size, ss))
+        return lambda: take(size, rs)
+
     def send(src, dst, ss, rs, to):
-        copy = pltpu.make_async_remote_copy(
-            src_ref=src, dst_ref=dst, send_sem=ss, recv_sem=rs, device_id=to, device_id_type=MESH
-        )
-        copy.start()
-        sent.append(copy)
-        return copy
+        push(src, dst, ss, rs, to)
+        return pushed(dst, ss, rs)
 
     own_rows = pl.ds(pl.multiple_of(r * OWN, OWN), OWN)
     loads = [
@@ -110,13 +118,14 @@
     pl.semaphore_wait(barrier, len(peers))
 
     zb[0] = slab[0]
-    zc = [
-        send(slab.at[(NZ - d) % 4], zb.at[NZ - d], zs.at[d], zrs.at[d], dev(x, y, zpeer(d), c)) for d in FAR[NZ]
-    ]
-    tc = [send(tgb.at[r], tgb.at[r], tss.at[k], trs.at[k], mates[k]) for k in range(GROUP - 1)]
-    uc = [
-        send(ub.at[own_rows, :], ub.at[own_rows, :], uss.at[k], urs.at[k], mates[k]) for k in range(GROUP - 1)
-    ]
+    for d in FAR[NZ]:
+        push(slab.at[(NZ - d) % 4], zb.at[NZ - d], zs.at[0], zs.at[1], dev(x, y, zpeer(d), c))
+    zc = pushed(zb.at[1:NZ], zs.at[0], zs.at[1])
+    for mate in mates:
+        push(tgb.at[r], tgb.at[r], tss.at[0], tss.at[1], mate)
+        push(ub.at[own_rows, :], ub.at[own_rows, :], uss.at[0], uss.at[1], mate)
+    tc = pushed(tgb.at[1:GROUP], tss.at[0], tss.at[1])
+    uc = pushed(ub.at[OWN:BLK, :], uss.at[0], uss.at[1])
 
     loads[3].wait()
     for l in range(LEVELS):
@@ -129,16 +138,15 @@
     zj = (z + 2 * (n % 4) + k // OWN) % NZ
     col[...] = (zj * 2 + c) * 2048 + (x * NY + (y + dy) % NY) * OWN + k % OWN
 
-    for cp in zc:
-        cp.wait_recv()
+    zc()
     halves = [(zb[k] + zb[k + 1]) + (zb[k + 2] + zb[k + 3]) for k in (0, 4)]
     yb[0] = jnp.concatenate(halves, axis=0).astype(BF16)
-    yc = {
-        NY - d: send(yb.at[0], yb.at[SLOT.index(NY - d)], yss.at[d], yrs.at[d], dev(x, ypeer(d), z, c))
-        for d in FAR[NY]
-    }
-    for cp in tc + uc:
-        cp.wait_recv()
+    for d in FAR[NY]:
+        at = SLOT.index(NY - d)
+        push(yb.at[0], yb.at[at], yss.at[0], yss.at[1 + at // (HALF // 4)], dev(x, ypeer(d), z, c))
+    sent.append((yb.at[1:NY], yss.at[0]))
+    tc()
+    uc()
     us[...] = (ub[...].astype(F32) * (D**-0.5)).astype(BF16)
     tsum = ((tgb[0] + tgb[1]) + (tgb[2] + tgb[3])) + ((tgb[4] + tgb[5]) + (tgb[6] + tgb[7]))
 
@@ -180,19 +188,15 @@
             mrun[rows] = m_new
             srun[rows] = s
 
-    def arrived(first, last):
-        for at in range(first, last):
-            yc[SLOT[at]].wait_recv()
-
     steps = len(SCORE) - 1
-    arrived(1, HALF // 4)
+    take(yb.at[1 : HALF // 4], yss.at[1])
     onehots(0)
     for j in range(steps + 2):
         if j < steps:
             vt[:, span(SCORE, j)] = dot(cbt[...], oh[:, span(SCORE, j)]).astype(BF16)
         if j + 1 < steps:
             if SCORE[j + 1] == HALF:
-                arrived(HALF // 4, NY)
+                take(yb.at[HALF // 4 : NY], yss.at[2])
             onehots(j + 1)
         if 1 <= j <= steps:
             lg[:, span(SCORE, j - 1)] = dot(us[...], vt[:, span(SCORE, j - 1)])
@@ -205,9 +209,9 @@
     s1 = jnp.sum(st * jnp.exp(mt - m1), axis=0, keepdims=True)
     quarters = [slice(q * LANES, (q + 1) * LANES) for q in range(BLK // LANES)]
     stat[r] = jnp.concatenate([m1[:, q] for q in quarters] + [s1[:, q] for q in quarters], axis=0)
-    sc = [send(stat.at[r], stat.at[r], sss.at[k], srs.at[k], mates[k]) for k in range(GROUP - 1)]
-    for cp in sc:
-        cp.wait_recv()
+    for mate in mates:
+        push(stat.at[r], stat.at[r], sss.at[0], sss.at[1], mate)
+    pushed(stat.at[1:GROUP], sss.at[0], sss.at[1])()
     ms = [stat[k][0:4] for k in range(GROUP)]
     top = ms[0]
     for k in range(1, GROUP):
@@ -260,24 +264,21 @@
     def block(at, rows):
         return pl.ds(pl.multiple_of(at * rows, 8), rows)
 
-    def done(copies):
-        for cp in copies:
-            cp.wait_recv()
-
     def scatter(l, a, src, into, rows, ss, rs):
         n = size[a]
         into[l, block(here[a], rows), :] = src[l, block(here[a], rows), :]
-        return [
-            send(
+        for d in FAR[n]:
+            push(
                 src.at[l, block(lax.rem(here[a] + d, n), rows), :], into.at[l, block(here[a], rows), :],
-                ss.at[l, d], rs.at[l, d], along(a, d),
+                ss.at[l], rs.at[l], along(a, d),
             )
-            for d in FAR[n]
-        ]
-
-    def spread(buf, pre, a, rows, ss, rs, sem):
+        return pushed(into.at[l, rows : n * rows, :], ss.at[l], rs.at[l])
+
+    def spread(buf, pre, a, rows, ss, rs):
         at = buf.at[pre + (block(here[a], rows), slice(None))]
-        return [send(at, at, ss.at[sem + (d,)], rs.at[sem + (d,)], along(a, d)) for d in FAR[size[a]]]
+        for d in FAR[size[a]]:
+            push(at, at, ss, rs, along(a, d))
+        return pushed(buf.at[pre + (slice(rows, size[a] * rows), slice(None))], ss, rs)
 
     def total(buf, pre, a, rows):
         parts = [buf[pre + (slice(k * rows, (k + 1) * rows), slice(None))] for k in range(size[a])]
@@ -288,53 +289,57 @@
     ways = (("y", "x", "z"), ("z", "x", "y"), ("x", "y", "z"))
 
     def first(l, cp):
-        cp.wait_recv()
+        cp()
         part[l] = cbuf[l, c] + dbuf[l]
         return scatter(l, ways[l][0], part, r1, K // size[ways[l][0]], s1s, s1r)
 
     def second(l, copies):
-        done(copies)
+        copies()
         a, b, _ = ways[l]
         rows = K // size[a]
         s2[l, 0:rows, :] = total(r1, (l,), a, rows)
         return scatter(l, b, s2, r2, 8, s2s, s2r)
 
     def third(l, copies):
-        done(copies)
+        copies()
         _, b, e = ways[l]
         r3[l, block(here[e], 8), :] = total(r2, (l,), b, 8)
-        return spread(r3, (l,), e, 8, s3s, s3r, (l,))
+        return spread(r3, (l,), e, 8, s3s.at[l], s3r.at[l])
 
     def fourth(l, copies):
-        done(copies)
+        copies()
         _, b, e = ways[l]
         a4[l, block(here[b], 8), :] = total(r3, (l,), e, 8)
-        return spread(a4, (l,), b, 8, s4s, s4r, (l,))
+        return spread(a4, (l,), b, 8, s4s.at[l], s4r.at[l])
 
     def fifth(l, copies):
-        done(copies)
+        copies()
         a = ways[l][0]
         rows = K // size[a]
         fin[c, l, block(here[a], rows), :] = a4[l, 0:rows, :]
-        return spread(fin, (c, l), a, rows, s5s, s5r, (l,))
-
-    def pass_on(l, at, rows, sem):
+        own = fin.at[c, l, block(here[a], rows), :]
+        for d in FAR[size[a]]:
+            push(own, own, s5s.at[l], s5r.at[l, d], along(a, d))
+        sent.append((fin.at[c, l, rows:K, :], s5s.at[l]))
+
+    def pass_on(l, at, rows):
         there = fin.at[c, l, block(at, rows), :]
-        return send(there, there, ds2.at[l, sem], dr2.at[l, sem], dev(x, y, z, 1 - c))
-
-    def last(l, copies):
+        push(there, there, ds2.at[l], dr2.at[l], dev(x, y, z, 1 - c))
+
+    def last(l):
         a = ways[l][0]
         n = size[a]
         rows = K // n
-        out = [pass_on(l, here[a], rows, 0)]
-        for d, cp in sorted(zip(FAR[n], copies), key=lambda t: min(t[0], n - t[0])):
-            cp.wait_recv()
-            out.append(pass_on(l, lax.rem(here[a] + n - d, n), rows, d))
-        return out
+        pass_on(l, here[a], rows)
+        for d in sorted(FAR[n], key=lambda d: min(d, n - d)):
+            at = lax.rem(here[a] + n - d, n)
+            take(fin.at[c, l, block(at, rows), :], s5r.at[l, d])
+            pass_on(l, at, rows)
+        return pushed(fin.at[1 - c, l], ds2.at[l], dr2.at[l])
 
     def loss_over(a, val, buf, ss, rs):
         buf[block(here[a], 8), :] = val
-        return spread(buf, (), a, 8, ss, rs, ())
+        return spread(buf, (), a, 8, ss.at[0], rs.at[0])
 
     d0 = level_out(0, w[0:K])
     own_lse = jnp.concatenate([lse * (1.0 / GROUP), jnp.zeros((4, LANES), F32)], axis=0)
@@ -344,7 +349,7 @@
     f0 = first(0, d0)
     d2 = level_out(2, w[2 * K :])
     f1 = first(1, d1)
-    ldc.wait_recv()
+    ldc()
     lxc = loss_over("x", ld[0] + ld[1], lx, lxs, lxr)
     f2 = first(2, d2)
     gu = dot_t(dl[...], vt[...]) * (D**-0.5)
@@ -353,39 +358,39 @@
     gdc = send(gus.at[:, 1 - c], gud, gds.at[0], gdr.at[0], dev(x, y, z, 1 - c))
     g0 = second(0, f0)
     g1 = second(1, f1)
-    done(lxc)
+    lxc()
     lyc = loss_over("y", total(lx, (), "x", 8), ly, lys, lyr)
     g2 = second(2, f2)
     h0 = third(0, g0)
     h1 = third(1, g1)
     h2 = third(2, g2)
-    done(lyc)
+    lyc()
     lzc = loss_over("z", total(ly, (), "y", 8), lz, lzs, lzr)
-    gdc.wait_recv()
+    gdc()
     gup[...] = gus[:, c] + gud[...]
     gur[x] = gup[x]
-    guc = [
-        send(gup.at[xpeer(d)], gur.at[x], gss.at[d], grs.at[d], dev(xpeer(d), y, z, c)) for d in FAR[NX]
-    ]
+    for d in FAR[NX]:
+        push(gup.at[xpeer(d)], gur.at[x], gss.at[0], gss.at[1], dev(xpeer(d), y, z, c))
+    guc = pushed(gur.at[1:NX], gss.at[0], gss.at[1])
     j0 = fourth(0, h0)
     j1 = fourth(1, h1)
     j2 = fourth(2, h2)
-    done(lzc)
+    lzc()
     loss_ref[...] = jnp.full((1, 1), jnp.sum(total(lz, (), "z", 8)) * (1.0 / USERS), F32)
-    done(guc)
+    guc()
     gu_ref[...] = (gur[0] + gur[1]) + (gur[2] + gur[3])
-    k0 = fifth(0, j0)
-    k1 = fifth(1, j1)
-    k2 = fifth(2, j2)
-    e2 = last(2, k2)
-    e0 = last(0, k0)
-    e1 = last(1, k1)
+    fifth(0, j0)
+    fifth(1, j1)
+    fifth(2, j2)
+    e2 = last(2)
+    e0 = last(0)
+    e1 = last(1)
     for l, copies in ((2, e2), (0, e0), (1, e1)):
-        done(copies)
+        copies()
         gc_ref[l, :, :LANES] = fin[0, l]
         gc_ref[l, :, LANES:] = fin[1, l]
-    for cp in sent:
-        cp.wait_send()
+    for at, sem in sent:
+        take(at, sem)
 
 
 def hand_over(gu_in, gc_in, loss_in, gu_ref, gc_ref, loss_ref):
@@ -412,11 +417,9 @@
         vmem((NX, 2, OWN, D), F32), vmem((NX, OWN, D), F32), vmem((NX, OWN, D), F32), vmem((NX, OWN, D), F32),
         vmem((2, 8, LANES), F32),
         vmem((NX * 8, LANES), F32), vmem((NY * 8, LANES), F32), vmem((NZ * 8, LANES), F32),
-        dma((4,)), dma((NZ,)), dma((NZ,)), dma((GROUP,)), dma((GROUP,)), dma((GROUP,)), dma((GROUP,)),
-        dma((NY,)), dma((NY,)), dma((GROUP,)), dma((GROUP,)),
-        dma((LEVELS,)), dma((LEVELS,)), *[dma((LEVELS, 8)) for _ in range(10)],
-        dma((LEVELS, 8)), dma((LEVELS, 8)), dma((1,)), dma((1,)), dma((NX,)), dma((NX,)),
-        dma((2,)), dma((2,)), dma((NX,)), dma((NX,)), dma((NY,)), dma((NY,)), dma((NZ,)), dma((NZ,)),
+        dma((4,)), dma((2,)), dma((2,)), dma((2,)), dma((3,)), dma((2,)),
+        dma((LEVELS,)), dma((LEVELS,)), *[dma((LEVELS,)) for _ in range(9)], dma((LEVELS, NY)),
+        dma((LEVELS,)), dma((LEVELS,)), dma((1,)), dma((1,)), dma((2,)), *[dma((1,)) for _ in range(8)],
     ]
     gu, gc, loss = pl.pallas_call(
         kernel,

time: 72.6 us -> 69.1 us (0.952)
  Pallas kernels: 71.8 us -> 68.3 us
    pallas_call x1, Pallas kernels: 69.1 us -> 65.7 us  [shards(): pl.pallas_call(kernel, out_shape=tuple((jax.ShapeDtypeStruct(n, F32) for...]
where the time goes in v5:
time: 69.1 us; the launch traced here: 69 us
  Pallas kernels  68.3 us (99%)
    pallas_call x1, Pallas kernels, shards(): pl.pallas_call(kernel, out_shape=tuple((jax.ShapeDtypeStruct(n, F32) for...  65.7 us
    pallas_call x1, Pallas kernels, shards(): pl.pallas_call(hand_over, out_shape=tuple((jax.ShapeDtypeStruct(n, F32) f...  2.67 us

profile of v5, /device:TPU:1, one launch (start us, length us, event | category | flops | bytes accessed | tf_op | source)
XLA Modules:
  0.0 69.0 jit_solution(11893786453870256427)
XLA Ops:
  0.6 65.7 %shard_map.67 = (f32[64,256]{1,0:T(8,128)}, f32[3,256,256]{2,1,0:T(8,128)}, f32[1,1]{1,0:T(1,128)}) custom-call(bf16[64,256]{1,0:T(8,128)(2,1)} %ue_hbm.1, s32[3,64]{1,0:T(4,128)} %codes_hbm.1, s32[1,64]{1,0:T(1,128)} %bitcast.4, bf16[768,256]{1,0:T(8,128)(2,1)} %bitcast.3), custom_call_target="tpu_custom_call" | custom-call | flops 8999999488 | bytes 2000000 | tf_op jit(solution)/shard_map/pallas_call | solution.py:424
  66.3 2.7 %shard_map.68 = (f32[64,256]{1,0:T(8,128)}, f32[3,256,256]{2,1,0:T(8,128)}, f32[1,1]{1,0:T(1,128)}) custom-call(f32[64,256]{1,0:T(8,128)} %get-tuple-element.9.gu_in, f32[3,256,256]{2,1,0:T(8,128)} %get-tuple-element.10.gc_in, f32[1,1]{1,0:T(1,128)} %get-tuple-element.11.loss_in), custom_call_target="tpu_custom_call" | custom-call | tf_op jit(solution)/shard_map/pallas_call | solution.py:435

commit v6 on v5

--- a/solution.py
+++ b/solution.py
@@ -40,9 +40,9 @@
     ub, us, cd, tg, slab, zb, yb, tgb, cb, cbt, iota_k, col,
     oh, vt, lg, dl, mrun, srun, stat, lsec, tcol, pos,
     cbuf, dbuf, part, r1, s2, r2, r3, a4, fin,
-    gus, gud, gup, gur, ld, lx, ly, lz,
+    gus, gud, gup, gur, guo, ld, lx, ly, lz,
     loc, zs, tss, uss, yss, sss,
-    ds, dr, s1s, s1r, s2s, s2r, s3s, s3r, s4s, s4r, s5s, s5r, ds2, dr2, gds, gdr, gss,
+    ds, dr, s1s, s1r, s2s, s2r, s3s, s3r, s4s, s4r, s5s, s5r, ds2, dr2, gds, gdr, gss, oss,
     lds, ldr, lxs, lxr, lys, lyr, lzs, lzr,
 ):
     u, i = lax.axis_index("user"), lax.axis_index("item")
@@ -286,7 +286,7 @@
             parts = [p + q for p, q in zip(parts[::2], parts[1::2])]
         return parts[0]
 
-    ways = (("y", "x", "z"), ("z", "x", "y"), ("x", "y", "z"))
+    ways = (("x", "z", "y"), ("y", "x", "z"), ("x", "y", "z"))
 
     def first(l, cp):
         cp()
@@ -378,7 +378,9 @@
     lzc()
     loss_ref[...] = jnp.full((1, 1), jnp.sum(total(lz, (), "z", 8)) * (1.0 / USERS), F32)
     guc()
-    gu_ref[...] = (gur[0] + gur[1]) + (gur[2] + gur[3])
+    guo[...] = (gur[0] + gur[1]) + (gur[2] + gur[3])
+    outs = [pltpu.make_async_copy(guo, gu_ref, oss.at[0, 0])]
+    outs[0].start()
     fifth(0, j0)
     fifth(1, j1)
     fifth(2, j2)
@@ -387,8 +389,14 @@
     e1 = last(1)
     for l, copies in ((2, e2), (0, e0), (1, e1)):
         copies()
-        gc_ref[l, :, :LANES] = fin[0, l]
-        gc_ref[l, :, LANES:] = fin[1, l]
+        for half in range(2):
+            out = pltpu.make_async_copy(
+                fin.at[half, l], gc_ref.at[l, :, half * LANES : (half + 1) * LANES], oss.at[half, l + 1]
+            )
+            out.start()
+            outs.append(out)
+    for out in outs:
+        out.wait()
     for at, sem in sent:
         take(at, sem)
 
@@ -415,17 +423,17 @@
         vmem((LEVELS, K, LANES), F32), vmem((LEVELS, 64, LANES), F32), vmem((LEVELS, 64, LANES), F32),
         vmem((LEVELS, 64, LANES), F32), vmem((LEVELS, 64, LANES), F32), vmem((2, LEVELS, K, LANES), F32),
         vmem((NX, 2, OWN, D), F32), vmem((NX, OWN, D), F32), vmem((NX, OWN, D), F32), vmem((NX, OWN, D), F32),
-        vmem((2, 8, LANES), F32),
+        vmem((OWN, D), F32), vmem((2, 8, LANES), F32),
         vmem((NX * 8, LANES), F32), vmem((NY * 8, LANES), F32), vmem((NZ * 8, LANES), F32),
         dma((4,)), dma((2,)), dma((2,)), dma((2,)), dma((3,)), dma((2,)),
         dma((LEVELS,)), dma((LEVELS,)), *[dma((LEVELS,)) for _ in range(9)], dma((LEVELS, NY)),
-        dma((LEVELS,)), dma((LEVELS,)), dma((1,)), dma((1,)), dma((2,)), *[dma((1,)) for _ in range(8)],
+        dma((LEVELS,)), dma((LEVELS,)), dma((1,)), dma((1,)), dma((2,)), dma((2, LEVELS + 1)), *[dma((1,)) for _ in range(8)],
     ]
     gu, gc, loss = pl.pallas_call(
         kernel,
         out_shape=tuple(jax.ShapeDtypeStruct(n, F32) for n in ((OWN, D), (LEVELS, K, D), (1, 1))),
         in_specs=[pl.BlockSpec(memory_space=pl.ANY)] * 4,
-        out_specs=[pl.BlockSpec(memory_space=vmem)] * 3,
+        out_specs=[pl.BlockSpec(memory_space=m) for m in (pl.ANY, pl.ANY, vmem)],
         scratch_shapes=scratch,
         compiler_params=pltpu.CompilerParams(
             collective_id=0, has_side_effects=True, vmem_limit_bytes=56 * 2**20

time: 69.1 us -> 69.5 us (level)
  no operation moved by 1% of the time
where the time goes in v6:
time: 69.5 us; the launch traced here: 69.3 us
  Pallas kernels  68.7 us (99%)
    pallas_call x1, Pallas kernels, shards(): pl.pallas_call(kernel, out_shape=tuple((jax.ShapeDtypeStruct(n, F32) for...  66 us
    pallas_call x1, Pallas kernels, shards(): pl.pallas_call(hand_over, out_shape=tuple((jax.ShapeDtypeStruct(n, F32) f...  2.67 us

profile of v6, /device:TPU:1, one launch (start us, length us, event | category | flops | bytes accessed | tf_op | source)
XLA Modules:
  0.0 69.3 jit_solution(14463019010468961497)
XLA Ops:
  0.6 66.0 %shard_map.67 = (f32[64,256]{1,0:T(8,128)}, f32[3,256,256]{2,1,0:T(8,128)}, f32[1,1]{1,0:T(1,128)}) custom-call(bf16[64,256]{1,0:T(8,128)(2,1)} %ue_hbm.1, s32[3,64]{1,0:T(4,128)} %codes_hbm.1, s32[1,64]{1,0:T(1,128)} %bitcast.4, bf16[768,256]{1,0:T(8,128)(2,1)} %bitcast.3), custom_call_target="tpu_custom_call" | custom-call | flops 8999999488 | bytes 2000000 | tf_op jit(solution)/shard_map/pallas_call | solution.py:432
  66.7 2.7 %shard_map.68 = (f32[64,256]{1,0:T(8,128)}, f32[3,256,256]{2,1,0:T(8,128)}, f32[1,1]{1,0:T(1,128)}) custom-call(f32[64,256]{1,0:T(8,128)} %get-tuple-element.9.gu_in, f32[3,256,256]{2,1,0:T(8,128)} %get-tuple-element.10.gc_in, f32[1,1]{1,0:T(1,128)} %get-tuple-element.11.loss_in), custom_call_target="tpu_custom_call" | custom-call | tf_op jit(solution)/shard_map/pallas_call | solution.py:443
